TPU v7x, 32 devices: a whole 2x2x4 slice. The times are simulated.
32 devices in a mesh: seq: 4 (over z), head: 8 (over y, x, core).
Axes of the slice: x: 2, y: 2, z: 4, core: 2. Of those that a mesh axis runs over, the one named last changes fastest.
Arguments:
- query: bfloat16 [32768, 2048], P('seq', 'head'), may hold values from -4.5 to 4.5
- keys: bfloat16 [32768, 2048], P('seq', 'head'), may hold values from -4.5 to 4.5
- values: bfloat16 [32768, 2048], P('seq', 'head'), may hold values from -6 to 6
- mem_init: float32 [16, 128, 128], P('head'), may hold values from -362.03867 to 362.03867
- beta: float32 [16], P('head'), may hold values from -2 to 2
- mem_gain: float32 [2048], P('head'), may hold values from 0.1 to 1.9
- loc_gain: float32 [2048], P('head'), may hold values from 0.1 to 1.9
- w_out: bfloat16 [2048, 2048], P('head'), may hold values from -0.125 to 0.125
Outputs:
- attn_out: bfloat16 [32768, 2048], P(('seq', 'head'))
- memory_prefix: float32 [4, 16, 128, 128], P('seq', 'head')
All inputs are finite; a program needn't handle non-finite values.
Results may differ from a plain program's by a relative error of at most 0.0054.
Values may be sent and summed in bfloat16 or wider, within the bound.
No kernel may reach another device: no remote copies, remote signals or barrier semaphores. Data moves between devices by JAX's collectives and lax.ppermute only.
A program may use at most 128 MiB of HBM per device.

v0:
```python
import functools

import jax
import jax.numpy as jnp
from jax import lax
from jax.experimental import pallas as pl
from jax.experimental.pallas import tpu as pltpu
from jax.sharding import PartitionSpec as P

HD = 128
SEG = 2048
BLOCK = 256
EPS = 1e-06
LOG2E = 1.4426950408889634
VMEM = 60 << 20
F32, BF16 = jnp.float32, jnp.bfloat16


def call(body, name, out_shape, grid_spec, flops, bytes_accessed, transcendentals=0):
    return pl.pallas_call(
        body,
        name=name,
        out_shape=out_shape,
        grid_spec=grid_spec,
        compiler_params=pltpu.CompilerParams(vmem_limit_bytes=VMEM),
        cost_estimate=pl.CostEstimate(
            flops=flops, bytes_accessed=bytes_accessed, transcendentals=transcendentals
        ),
    )


def whole(shape, memory_space=pltpu.VMEM):
    return pl.BlockSpec(shape, lambda *_: (0,) * len(shape), memory_space=memory_space)


def elu_feature(source):
    wide = source.astype(F32)
    return jnp.where(wide > 0, wide + 1.0, jnp.exp(wide)).astype(BF16)


def columns(head):
    return slice(head * HD, (head + 1) * HD)


def kv_body(k_ref, v_ref, term_ref, total_ref):
    for head in range(k_ref.shape[1] // HD):
        cols = columns(head)
        term = lax.dot_general(
            elu_feature(k_ref[:, cols]),
            v_ref[:, cols],
            (((0,), (0,)), ((), ())),
            preferred_element_type=F32,
        )
        term_ref[0, head] = term

        total_ref[head] = jnp.where(pl.program_id(0) == 0, 0.0, total_ref[head]) + term


def kv_terms(keys, values):
    tokens, width = keys.shape
    heads, segs = width // HD, tokens // SEG
    block = pl.BlockSpec((SEG, width), lambda seg: (seg, 0))
    return call(
        kv_body,
        "kv_terms",
        (
            jax.ShapeDtypeStruct((segs, heads, HD, HD), F32),
            jax.ShapeDtypeStruct((heads, HD, HD), F32),
        ),
        pl.GridSpec(
            grid=(segs,),
            in_specs=[block, block],
            out_specs=[
                pl.BlockSpec((1, heads, HD, HD), lambda seg: (seg, 0, 0, 0)),
                whole((heads, HD, HD)),
            ],
        ),
        2 * tokens * width * HD,
        2 * keys.size * 2,
    )(keys, values)


def mean_square(source):
    return jnp.mean(source * source, axis=-1, keepdims=True)


def scores_of(q, k):
    rows, end = q.shape[0], k.shape[0]
    wide = q.astype(F32) * (HD**-0.5 * LOG2E)
    high = wide.astype(BF16)
    low = (wide - high.astype(F32)).astype(BF16)
    scores = lax.dot_general(
        jnp.concatenate([high, low], axis=1),
        jnp.concatenate([k, k], axis=1),
        (((1,), (1,)), ((), ())),
        preferred_element_type=F32,
    )
    row = lax.broadcasted_iota(jnp.int32, (rows, rows), 0)
    col = lax.broadcasted_iota(jnp.int32, (rows, rows), 1)
    diagonal = jnp.where(col <= row, scores[:, end - rows :], -jnp.inf)
    if end > rows:
        return jnp.concatenate([scores[:, : end - rows], diagonal], axis=1)
    return diagonal


def local_branch(scores, v, scale_gain):
    largest = jnp.max(scores, axis=-1, keepdims=True)
    weights = jnp.exp2(scores - largest).astype(BF16)
    summed = jnp.dot(
        weights, jnp.concatenate([v, jnp.ones_like(v)], axis=1), preferred_element_type=F32
    )
    local, denominator = summed[:, :HD], summed[:, HD:]
    return local * (
        lax.rsqrt(mean_square(local) + EPS * denominator * denominator) * scale_gain
    )


def score_ahead(units, q_ref, k_ref, use):
    def make(unit):
        dest, at, _, end, head = unit
        return scores_of(q_ref[0, dest, at, :, columns(head)], k_ref[:end, columns(head)])

    ahead = make(units[0])
    for unit, following in zip(units, [*units[1:], None]):
        scores = ahead
        if following is not None:
            ahead = make(following)
        use(unit, scores)


def memory_branch(q, memory_pair, scale_gain):
    both = jnp.dot(elu_feature(q), memory_pair, preferred_element_type=F32)
    read = both[:, :HD] + both[:, HD:]
    return read * (lax.rsqrt(mean_square(read) + EPS) * scale_gain)


def gate_of(beta_ref, head):
    return 1.0 / (1.0 + jnp.exp(-jnp.full((1, HD), beta_ref[head], F32)))


def chunk_blocks(dests, blocks, per_dest):
    for dest in range(dests):
        for at, block in enumerate(blocks):
            start = (dest * per_dest + block) * BLOCK
            yield dest, at, slice(at * BLOCK, (at + 1) * BLOCK), start + BLOCK


def units_of(dests, blocks, per_dest, heads):
    return [
        (*found, head) for found in chunk_blocks(dests, blocks, per_dest) for head in range(heads)
    ]


def local_body(blocks, per_dest, q_ref, k_ref, v_ref, beta_ref, gain_ref, out_ref):
    _, dests, _, _, width = q_ref.shape

    def use(unit, scores):
        dest, _, rows, end, head = unit
        cols = columns(head)
        out_ref[dest, rows, cols] = local_branch(
            scores, v_ref[:end, cols], (1.0 - gate_of(beta_ref, head)) * gain_ref[:, cols]
        )

    score_ahead(units_of(dests, blocks, per_dest, width // HD), q_ref, k_ref, use)


def advance_memory(base_ref, term_ref, memory):
    @pl.when(pl.program_id(0) == 0)
    def _():
        memory[...] = base_ref[...]

    pairs = []
    for head in range(memory.shape[0]):
        now = memory[head]
        high = now.astype(BF16)
        low = (now - high.astype(F32)).astype(BF16)
        pairs.append(jnp.concatenate([high, low], axis=1))
        memory[head] = now + term_ref[0, head]
    return pairs


def mix_body(blocks, per_dest, q_ref, local_ref, base_ref, term_ref, beta_ref, gain_ref, out_ref, memory):
    _, dests, _, _, width = q_ref.shape
    pairs = advance_memory(base_ref, term_ref, memory)
    for dest, at, rows, _ in chunk_blocks(dests, blocks, per_dest):
        for head, pair in enumerate(pairs):
            cols = columns(head)
            read = memory_branch(
                q_ref[0, dest, at, :, cols], pair, gate_of(beta_ref, head) * gain_ref[:, cols]
            )
            out_ref[dest, rows, cols] = (read + local_ref[dest, rows, cols]).astype(BF16)


def both_body(
    blocks,
    per_dest,
    q_ref,
    k_ref,
    v_ref,
    base_ref,
    term_ref,
    beta_ref,
    mem_gain_ref,
    loc_gain_ref,
    *rest,
):
    *_, out_ref, memory = rest
    _, dests, _, _, width = q_ref.shape
    pairs = advance_memory(base_ref, term_ref, memory)

    def use(unit, scores):
        dest, at, rows, end, head = unit
        cols = columns(head)
        gate = gate_of(beta_ref, head)
        local = local_branch(scores, v_ref[:end, cols], (1.0 - gate) * loc_gain_ref[:, cols])
        read = memory_branch(q_ref[0, dest, at, :, cols], pairs[head], gate * mem_gain_ref[:, cols])
        out_ref[dest, rows, cols] = (read + local).astype(BF16)

    score_ahead(units_of(dests, blocks, per_dest, width // HD), q_ref, k_ref, use)


def chunk_call(kind, blocks, dests, query, arrays, after=()):
    tokens, width = query.shape
    segs, heads = tokens // SEG, width // HD
    per_dest = SEG // dests // BLOCK
    size = len(blocks) * BLOCK
    q = query.reshape(segs, dests, per_dest, BLOCK, width)
    specs = [
        pl.BlockSpec(
            (pl.Element(1), pl.Element(dests), pl.Element(len(blocks)), pl.Element(BLOCK), pl.Element(width)),
            lambda seg: (seg, 0, blocks[0], 0, 0),
        )
    ]
    for array in arrays:
        if array.shape == query.shape:
            specs.append(pl.BlockSpec((SEG, width), lambda seg: (seg, 0)))
        elif array.ndim == 1:
            specs.append(pl.BlockSpec(memory_space=pltpu.SMEM))
        elif array.ndim == 4:
            specs.append(pl.BlockSpec((1, heads, HD, HD), lambda seg: (seg, 0, 0, 0)))
        elif array.shape[1:] == (size, width):
            specs.append(pl.BlockSpec((dests, size, width), lambda seg: (seg, 0, 0)))
        else:
            specs.append(whole(array.shape))
    specs.extend([pl.BlockSpec(memory_space=pl.ANY)] * len(after))
    body = {"local": local_body, "mix": mix_body, "both": both_body}[kind]
    keys_met = segs * sum(end for *_, end in chunk_blocks(dests, blocks, per_dest))
    cost = dict(
        flops=8 * keys_met * BLOCK * width, bytes_accessed=6 * tokens * width, transcendentals=keys_met * BLOCK * heads
    )
    if kind == "mix":
        cost = dict(flops=8 * segs * dests * size * width * HD, bytes_accessed=8 * segs * dests * size * width)
    return call(
        functools.partial(body, blocks, per_dest),
        f"attention_{kind}",
        jax.ShapeDtypeStruct((segs * dests, size, width), F32 if kind == "local" else BF16),
        pl.GridSpec(
            grid=(segs,),
            in_specs=specs,
            out_specs=pl.BlockSpec((dests, size, width), lambda seg: (seg, 0, 0)),
            scratch_shapes=[] if kind == "local" else [pltpu.VMEM((heads, HD, HD), F32)],
        ),
        **cost,
    )(q, *arrays, *after)


def flip(array, axis, size, turn):
    return lax.ppermute(array, axis, [(at, at ^ turn) for at in range(size)])


class RowGather:
    def __init__(self, w_out, seq_size, head_size):
        half = w_out.shape[0] // 2
        self.seq_size, self.head_size = seq_size, head_size
        self.paired = seq_size % 2 == 0 and half % HD == 0
        own = w_out
        if self.paired:
            own = lax.dynamic_slice_in_dim(w_out, lax.axis_index("seq") % 2 * half, half, 0)
        self.pieces = {0: [w_out]}
        self.own = own

    def near(self):
        for turn in range(2, self.head_size, 2):
            self.pieces[turn] = [flip(self.own, "head", self.head_size, turn)]
        self.across(0)

    def swap(self, turn):
        if self.paired:
            self.pieces[turn].append(flip(self.pieces[turn][0], "seq", self.seq_size, 1))

    def across(self, turn):
        done = self.pieces.setdefault(turn + 1, [])
        for piece in self.pieces[turn][len(done) :]:
            done.append(flip(piece, "head", self.head_size, 1))

    def now(self, *turns):
        return [piece for turn in turns for piece in self.pieces[turn]]

    def all(self):
        return [tuple(self.pieces[turn]) for turn in range(self.head_size)]


def project_body(place_ref, *refs, count, parts_of):
    row_refs, w_refs, out_ref = refs[:count], refs[count : count + sum(parts_of)], refs[-1]
    width = row_refs[0].shape[2]
    rows = []
    for row_ref in row_refs:
        found = []
        for turn, parts in enumerate(parts_of):
            source, size = place_ref[0] ^ turn, width // parts
            for part in range(parts):
                place = part if parts == 1 else place_ref[1] ^ part
                cols = pl.ds(pl.multiple_of(place * size, size), size)
                found.append(row_ref[source, :, cols])
        rows.append(jnp.concatenate(found, axis=1))
    w_all = jnp.concatenate([w_ref[...] for w_ref in w_refs], axis=0)
    out_ref[...] = jnp.dot(
        jnp.concatenate(rows, axis=0), w_all, preferred_element_type=F32
    ).astype(BF16)


def project(place, chunks, pieces, first, tokens, so_far=None):
    sources, _, width = chunks[0].shape
    count = sum(chunk.shape[1] for chunk in chunks)
    flat, parts_of = [], []
    for piece in pieces:
        parts = piece if isinstance(piece, tuple) else (piece,)
        flat.extend(parts)
        parts_of.append(len(parts))
    depth, out_width = width * sources, flat[0].shape[1]
    strip = min(512, out_width)
    specs = [whole(chunk.shape) for chunk in chunks]
    specs += [pl.BlockSpec((part.shape[0], strip), lambda at, _: (0, at)) for part in flat]
    specs += [pl.BlockSpec(memory_space=pl.ANY)] * (so_far is not None)
    extra = () if so_far is None else (so_far,)
    return pl.pallas_call(
        functools.partial(project_body, count=len(chunks), parts_of=tuple(parts_of)),
        name="project",
        out_shape=jax.ShapeDtypeStruct((tokens, out_width), BF16),
        grid_spec=pltpu.PrefetchScalarGridSpec(
            num_scalar_prefetch=1,
            grid=(out_width // strip,),
            in_specs=specs,
            out_specs=pl.BlockSpec(
                (pl.Element(count), pl.Element(strip)), lambda at, _: (first, at * strip)
            ),
        ),
        input_output_aliases={} if so_far is None else {len(specs): 0},
        compiler_params=pltpu.CompilerParams(vmem_limit_bytes=VMEM),
        cost_estimate=pl.CostEstimate(
            flops=2 * count * depth * out_width,
            bytes_accessed=2 * (count * depth + depth * out_width + count * out_width),
            transcendentals=0,
        ),
    )(place, *chunks, *flat, *extra)


def per_device(
    sizes, query, keys, values, mem_init, beta, mem_gain, loc_gain, w_out
):
    seq_size, head_size = sizes
    tokens, width = query.shape
    dests = head_size * SEG // tokens
    per_dest = SEG // dests // BLOCK
    place = jnp.stack([lax.axis_index("head"), lax.axis_index("seq") % 2]).astype(jnp.int32)
    mem_gain, loc_gain = mem_gain.reshape(1, width), loc_gain.reshape(1, width)

    gather = RowGather(w_out, seq_size, head_size)
    gather.near()
    terms, total = kv_terms(keys, values)
    memory_base = mem_init
    for step in range(1, seq_size):
        memory_base = memory_base + lax.ppermute(
            total, "seq", [(at, at + step) for at in range(seq_size - step)]
        )
    memory_prefix = (memory_base * tokens ** (-0.5))[None]

    if per_dest > 2:
        groups = [(0,), tuple(range(1, per_dest - 1)), (per_dest - 1,)]
    else:
        groups = [(at,) for at in range(per_dest)]
    *near, last = range(2, head_size, 2)
    arrived, after = [], ()
    for blocks in groups:
        run = functools.partial(chunk_call, blocks=blocks, dests=dests, query=query)
        if blocks == groups[0]:
            local = run("local", arrays=[keys, values, beta, loc_gain])
            chunk = run("mix", arrays=[local, memory_base, terms, beta, mem_gain])
            after = gather.now(1, *near)
        else:
            chunk = run(
                "both",
                arrays=[keys, values, memory_base, terms, beta, mem_gain, loc_gain],
                after=tuple(after),
            )
        if blocks == groups[1]:
            for turn in near:
                gather.across(turn)
            after = gather.now(*[turn + 1 for turn in near])
            gather.swap(near[0])
            chunk, early = lax.optimization_barrier((chunk, gather.now(near[0], last)))
            gather.pieces[last] = [early.pop()]
            gather.pieces[near[0]] = early
            for turn in near[1:]:
                gather.swap(turn)
        if blocks == groups[-1]:
            turns = (*near, last)
            _, held = lax.optimization_barrier((chunk, [gather.pieces[turn] for turn in turns]))
            gather.pieces.update(zip(turns, held))
            gather.swap(last)
            for turn in turns:
                gather.across(turn)
        arrived.append(lax.all_to_all(chunk, "head", split_axis=0, concat_axis=0, tiled=True))
    pieces = gather.all()
    rows = tokens // head_size
    last = len(groups[-1]) * BLOCK
    out = project(place, arrived[:-1], pieces, 0, rows)
    out = project(place, arrived[-1:], pieces, rows - last, rows, out)
    return out, memory_prefix


def solution(mesh):
    sizes = (mesh.shape["seq"], mesh.shape["head"])
    in_specs = (
        P("seq", "head"),
        P("seq", "head"),
        P("seq", "head"),
        P("head", None, None),
        P("head"),
        P("head"),
        P("head"),
        P("head", None),
    )
    out_specs = (P(("seq", "head"), None), P("seq", "head", None, None))
    return jax.shard_map(
        functools.partial(per_device, sizes),
        mesh=mesh,
        in_specs=in_specs,
        out_specs=out_specs,
        check_vma=False,
    )
```

profile of v0, /device:TPU:24, one launch (start us, length us, event | category | flops | bytes accessed | tf_op | source)
XLA Modules:
  0.0 124.7 jit_solution(9907645262052303963)
XLA Ops:
  0.7 6.1 %kv_terms.1 = (f32[4,2,128,128]{3,2,1,0:T(8,128)}, f32[2,128,128]{2,1,0:T(8,128)}) custom-call(bf16[8192,256]{1,0:T(8,128)(2,1)} %k_ref.7, bf16[8192,256]{1,0:T(8,128)(2,1)} %v_ref.7), custom_call_target="tpu_custom_call" | custom-call | flops 536870912 | bytes 8388608 | tf_op jit(solution)/shard_map/kv_terms/pallas_call | solution.py:63
  6.8 1.3 %collective-permute-start.2 = (f32[2,128,128]{2,1,0:T(8,128)}, f32[2,128,128]{2,1,0:T(8,128)S(1)}, u32[]{:S(2)}, u32[]{:S(2)}) collective-permute-start(f32[2,128,128]{2,1,0:T(8,128)} %get-tuple-element.13), channel_id=1, source_target_pairs={{0,24},{1,25},{2,26},{3,27},{4,28},{5,29},{6,30},{7,31}} | collective-permute-start | bytes 393224 | tf_op jit(solution)/shard_map/ppermute | solution.py:373
  8.1 0.8 constant_dynamic-slice_fusion
  9.0 1.5 %collective-permute-start.5 = (bf16[128,2048]{1,0:T(8,128)(2,1)}, bf16[128,2048]{1,0:T(8,128)(2,1)}, u32[]{:S(2)}, u32[]{:S(2)}) collective-permute-start(bf16[128,2048]{1,0:T(8,128)(2,1)} %constant_dynamic-slice_fusion), channel_id=1, source_target_pairs={{0,4},{1,5},{2,6},{3,7},{4,0},{5,1},{6,2},{7,3},{8,12},{9,13},{10,... | collective-permute-start | bytes 1572872 | tf_op jit(solution)/shard_map/ppermute | solution.py:268
  10.5 1.5 %collective-permute-start.3 = (bf16[128,2048]{1,0:T(8,128)(2,1)}, bf16[128,2048]{1,0:T(8,128)(2,1)S(1)}, u32[]{:S(2)}, u32[]{:S(2)}) collective-permute-start(bf16[128,2048]{1,0:T(8,128)(2,1)} %constant_dynamic-slice_fusion), channel_id=1, source_target_pairs={{0,2},{1,3},{2,0},{3,1},{4,6},{5,7},{6,4},{7,5},{8,10},{9,11},{10,... | collective-permute-start | bytes 1572872 | tf_op jit(solution)/shard_map/ppermute | solution.py:268
  12.0 1.3 %collective-permute-start.1 = (f32[2,128,128]{2,1,0:T(8,128)}, f32[2,128,128]{2,1,0:T(8,128)S(1)}, u32[]{:S(2)}, u32[]{:S(2)}) collective-permute-start(f32[2,128,128]{2,1,0:T(8,128)} %get-tuple-element.13), channel_id=1, source_target_pairs={{0,16},{8,24},{1,17},{9,25},{2,18},{10,26},{3,19},{11,27},{4,20},{... | collective-permute-start | bytes 393224 | tf_op jit(solution)/shard_map/ppermute | solution.py:373
  13.3 3.3 %collective-permute-done.2 = f32[2,128,128]{2,1,0:T(8,128)S(1)} collective-permute-done((f32[2,128,128]{2,1,0:T(8,128)}, f32[2,128,128]{2,1,0:T(8,128)S(1)}, u32[]{:S(2)}, u32[]{:S(2)}) %collective-permute-start.2) | collective-permute-done | bytes 131104 | tf_op jit(solution)/shard_map/ppermute | solution.py:373
  16.5 1.3 %collective-permute-start = (f32[2,128,128]{2,1,0:T(8,128)}, f32[2,128,128]{2,1,0:T(8,128)S(1)}, u32[]{:S(2)}, u32[]{:S(2)}) collective-permute-start(f32[2,128,128]{2,1,0:T(8,128)} %get-tuple-element.13), channel_id=1, source_target_pairs={{0,8},{8,16},{16,24},{1,9},{9,17},{17,25},{2,10},{10,18},{18,26},{... | collective-permute-start | bytes 393224 | tf_op jit(solution)/shard_map/ppermute | solution.py:373
  17.8 8.8 %attention_local.1.local_ref = f32[8,256,256]{2,1,0:T(8,128)} custom-call(bf16[4,2,4,256,256]{4,3,2,1,0:T(8,128)(2,1)} %bitcast.7, bf16[8192,256]{1,0:T(8,128)(2,1)} %k_ref.7, bf16[8192,256]{1,0:T(8,128)(2,1)} %v_ref.7, f32[2]{0:T(128)} %beta_ref.7, f32[1,256]{1,0:T(1,128)} %bitcast.14), custom_call_target="tpu_custom_call" | custom-call | flops 3221225472 | bytes 12582912 | tf_op jit(solution)/shard_map/attention_local/pallas_call | solution.py:253
  26.7 0.7 multiply_bitcast_fusion
  27.4 4.7 %attention_mix.1 = bf16[8,256,256]{2,1,0:T(8,128)(2,1)} custom-call(bf16[4,2,4,256,256]{4,3,2,1,0:T(8,128)(2,1)} %bitcast.8, f32[8,256,256]{2,1,0:T(8,128)} %attention_local.1.local_ref, f32[2,128,128]{2,1,0:T(8,128)} %get-tuple-element.25.base_ref, f32[4,2,128,128]{3,2,1,0:T(8,128)} %get-tuple-element.14.term_ref, f32[2]{0:T(128)} %beta_ref.7, ...), custom_call_target="tpu_custom_call" | custom-call | flops 536870912 | bytes 4194304 | tf_op jit(solution)/shard_map/attention_mix/pallas_call | solution.py:253
  32.1 3.9 %all-to-all-start.1 = ((bf16[8,256,256]{2,1,0:T(8,128)(2,1)}), bf16[8,256,256]{2,1,0:T(8,128)(2,1)S(1)}, u32[]{:S(2)}, u32[]{:S(2)}) async-start(bf16[8,256,256]{2,1,0:T(8,128)(2,1)} %attention_mix.1), calls=%async_computation.1 | async-start | bytes 2097152 | tf_op jit(solution)/shard_map/all_to_all | solution.py:413
  36.0 2.9 %collective-permute-start.9 = (bf16[128,2048]{1,0:T(8,128)(2,1)}, bf16[128,2048]{1,0:T(8,128)(2,1)}, u32[]{:S(2)}, u32[]{:S(2)}) collective-permute-start(bf16[128,2048]{1,0:T(8,128)(2,1)} %constant_dynamic-slice_fusion), channel_id=1, source_target_pairs={{0,6},{1,7},{2,4},{3,5},{4,2},{5,3},{6,0},{7,1},{8,14},{9,15},{10,... | collective-permute-start | bytes 1572872 | tf_op jit(solution)/shard_map/ppermute | solution.py:268
  38.9 2.6 %collective-permute-start.8 = (bf16[128,2048]{1,0:T(8,128)(2,1)S(1)}, bf16[128,2048]{1,0:T(8,128)(2,1)}, u32[]{:S(2)}, u32[]{:S(2)}) collective-permute-start(bf16[128,2048]{1,0:T(8,128)(2,1)S(1)} %collective-permute-done.3.rest_1_.refs_4_.refs_3_), channel_id=1, source_target_pairs={{0,8},{8,0},{16,24},{24,16},{1,9},{9,1},{17,25},{25,17},{2,10},{10... | collective-permute-start | bytes 1572872 | tf_op jit(solution)/shard_map/ppermute | solution.py:268
  41.6 0.5 collective-permute-start.6
  42.1 1.0 copy-done.3
  43.1 17.2 %attention_both.3 = bf16[8,512,256]{2,1,0:T(8,128)(2,1)} custom-call(bf16[4,2,4,256,256]{4,3,2,1,0:T(8,128)(2,1)} %bitcast.9, bf16[8192,256]{1,0:T(8,128)(2,1)} %k_ref.7, bf16[8192,256]{1,0:T(8,128)(2,1)} %v_ref.7, f32[2,128,128]{2,1,0:T(8,128)} %get-tuple-element.25.base_ref, f32[4,2,128,128]{3,2,1,0:T(8,128)} %get-tuple-element.14.term_ref, f32[2]{0:T(128)} %beta_ref.7, ...), custom_call_target="tpu_custom_call" | custom-call | flops 9663676416 | bytes 12582912 | tf_op jit(solution)/shard_map/attention_both/pallas_call | solution.py:253
  60.2 2.5 %collective-permute-done.9.refs_12_.refs_11_ = bf16[128,2048]{1,0:T(8,128)(2,1)} collective-permute-done((bf16[128,2048]{1,0:T(8,128)(2,1)}, bf16[128,2048]{1,0:T(8,128)(2,1)}, u32[]{:S(2)}, u32[]{:S(2)}) %collective-permute-start.9) | collective-permute-done | bytes 524320 | tf_op jit(solution)/shard_map/ppermute | solution.py:268
  62.8 1.0 copy-done.4
  63.7 3.6 %all-to-all-start.2 = ((bf16[8,512,256]{2,1,0:T(8,128)(2,1)}), bf16[8,512,256]{2,1,0:T(8,128)(2,1)S(1)}, u32[]{:S(2)}, u32[]{:S(2)}) async-start(bf16[8,512,256]{2,1,0:T(8,128)(2,1)} %attention_both.3), calls=%async_computation.2 | async-start | bytes 4194304 | tf_op jit(solution)/shard_map/all_to_all | solution.py:413
  67.3 2.7 %collective-permute-start.10 = (bf16[128,2048]{1,0:T(8,128)(2,1)}, bf16[128,2048]{1,0:T(8,128)(2,1)}, u32[]{:S(2)}, u32[]{:S(2)}) collective-permute-start(bf16[128,2048]{1,0:T(8,128)(2,1)} %collective-permute-done.5.rest_2_.refs_8_.refs_7_), channel_id=1, source_target_pairs={{0,8},{8,0},{16,24},{24,16},{1,9},{9,1},{17,25},{25,17},{2,10},{10... | collective-permute-start | bytes 1572872 | tf_op jit(solution)/shard_map/ppermute | solution.py:268
  70.0 0.8 copy-done.6
  70.9 11.8 %attention_both.2 = bf16[8,256,256]{2,1,0:T(8,128)(2,1)} custom-call(bf16[4,2,4,256,256]{4,3,2,1,0:T(8,128)(2,1)} %bitcast.10, bf16[8192,256]{1,0:T(8,128)(2,1)} %k_ref.7, bf16[8192,256]{1,0:T(8,128)(2,1)} %v_ref.7, f32[2,128,128]{2,1,0:T(8,128)} %get-tuple-element.25.base_ref, f32[4,2,128,128]{3,2,1,0:T(8,128)} %get-tuple-element.14.term_ref, f32[2]{0:T(128)} %beta_ref.7, ...), custom_call_target="tpu_custom_call" | custom-call | flops 6442450944 | bytes 12582912 | tf_op jit(solution)/shard_map/attention_both/pallas_call | solution.py:253
  82.8 1.7 %collective-permute-start.13 = (bf16[128,2048]{1,0:T(8,128)(2,1)}, bf16[128,2048]{1,0:T(8,128)(2,1)}, u32[]{:S(2)}, u32[]{:S(2)}) collective-permute-start(bf16[128,2048]{1,0:T(8,128)(2,1)} %collective-permute-done.9.refs_12_.refs_11_), channel_id=1, source_target_pairs={{0,8},{8,0},{16,24},{24,16},{1,9},{9,1},{17,25},{25,17},{2,10},{10... | collective-permute-start | bytes 1572872 | tf_op jit(solution)/shard_map/ppermute | solution.py:268
  84.5 0.5 collective-permute-start.11
  85.0 11.9 %collective-permute-done.13.refs_13_.refs_12_ = bf16[128,2048]{1,0:T(8,128)(2,1)} collective-permute-done((bf16[128,2048]{1,0:T(8,128)(2,1)}, bf16[128,2048]{1,0:T(8,128)(2,1)}, u32[]{:S(2)}, u32[]{:S(2)}) %collective-permute-start.13) | collective-permute-done | bytes 524320 | tf_op jit(solution)/shard_map/ppermute | solution.py:268
  97.0 4.0 %all-to-all-start = ((bf16[8,256,256]{2,1,0:T(8,128)(2,1)}), bf16[8,256,256]{2,1,0:T(8,128)(2,1)S(1)}, u32[]{:S(2)}, u32[]{:S(2)}) async-start(bf16[8,256,256]{2,1,0:T(8,128)(2,1)} %attention_both.2), calls=%async_computation | async-start | bytes 2097152 | tf_op jit(solution)/shard_map/all_to_all | solution.py:413
  101.0 0.6 pad_add_fusion.place_ref
  101.6 11.6 %project.2.refs_15_ = bf16[1024,2048]{1,0:T(8,128)(2,1)} custom-call(s32[2]{0:T(128)} %pad_add_fusion.place_ref, bf16[8,256,256]{2,1,0:T(8,128)(2,1)} %copy-done.4, bf16[8,512,256]{2,1,0:T(8,128)(2,1)} %copy-done.2, bf16[256,2048]{1,0:T(8,128)(2,1)} %refs_1_.1, bf16[256,2048]{1,0:T(8,128)(2,1)} %copy-done.3, bf16[128,2048]{1,0:T(8,128)(2,1)} %copy-done.5, ...), custom_call_target="tpu_custom_call" | custom-call | flops 6442450944 | bytes 14680064 | tf_op jit(solution)/shard_map/project/pallas_call | solution.py:336
  113.2 3.2 %all-to-all-done.refs_0_ = bf16[8,256,256]{2,1,0:T(8,128)(2,1)S(1)} async-done(((bf16[8,256,256]{2,1,0:T(8,128)(2,1)}), bf16[8,256,256]{2,1,0:T(8,128)(2,1)S(1)}, u32[]{:S(2)}, u32[]{:S(2)}) %all-to-all-start) | async-done | bytes 1048608 | tf_op jit(solution)/shard_map/all_to_all | solution.py:413
  116.4 1.0 copy-done
  117.3 7.3 %project.3 = bf16[1024,2048]{1,0:T(8,128)(2,1)} custom-call(s32[2]{0:T(128)} %pad_add_fusion.place_ref, bf16[8,256,256]{2,1,0:T(8,128)(2,1)} %copy-done, bf16[256,2048]{1,0:T(8,128)(2,1)} %refs_1_.1, bf16[256,2048]{1,0:T(8,128)(2,1)} %copy-done.3, bf16[128,2048]{1,0:T(8,128)(2,1)} %copy-done.5, ...), custom_call_target="tpu_custom_call", output_to_operand_aliasing={{}: (16, {})} | custom-call | flops 2147483648 | bytes 10485760 | tf_op jit(solution)/shard_map/project/pallas_call | solution.py:336
  (32 shorter events, 0.2 us)
Async XLA Ops:
  0.6 7.5 %copy-start.1 = (bf16[256,2048]{1,0:T(8,128)(2,1)S(1)}, bf16[256,2048]{1,0:T(8,128)(2,1)}, u32[]{:S(2)}) copy-start(bf16[256,2048]{1,0:T(8,128)(2,1)} %refs_1_.1) | copy-start | bytes 3145732
  0.6 41.4 %collective-permute-start.7 = (bf16[256,2048]{1,0:T(8,128)(2,1)}, bf16[256,2048]{1,0:T(8,128)(2,1)S(1)}, u32[]{:S(2)}, u32[]{:S(2)}) collective-permute-start(bf16[256,2048]{1,0:T(8,128)(2,1)} %refs_1_.1), channel_id=1, source_target_pairs={{0,1},{1,0},{2,3},{3,2},{4,5},{5,4},{6,7},{7,6},{8,9},{9,8},{10,11... | collective-permute-start | bytes 3145736 | tf_op jit(solution)/shard_map/ppermute | solution.py:268
  6.8 9.7 %collective-permute-start.2 = (f32[2,128,128]{2,1,0:T(8,128)}, f32[2,128,128]{2,1,0:T(8,128)S(1)}, u32[]{:S(2)}, u32[]{:S(2)}) collective-permute-start(f32[2,128,128]{2,1,0:T(8,128)} %get-tuple-element.13), channel_id=1, source_target_pairs={{0,24},{1,25},{2,26},{3,27},{4,28},{5,29},{6,30},{7,31}} | collective-permute-start | bytes 393224 | tf_op jit(solution)/shard_map/ppermute | solution.py:373
  9.0 32.6 %collective-permute-start.5 = (bf16[128,2048]{1,0:T(8,128)(2,1)}, bf16[128,2048]{1,0:T(8,128)(2,1)}, u32[]{:S(2)}, u32[]{:S(2)}) collective-permute-start(bf16[128,2048]{1,0:T(8,128)(2,1)} %constant_dynamic-slice_fusion), channel_id=1, source_target_pairs={{0,4},{1,5},{2,6},{3,7},{4,0},{5,1},{6,2},{7,3},{8,12},{9,13},{10,... | collective-permute-start | bytes 1572872 | tf_op jit(solution)/shard_map/ppermute | solution.py:268
  10.5 28.4 %collective-permute-start.3 = (bf16[128,2048]{1,0:T(8,128)(2,1)}, bf16[128,2048]{1,0:T(8,128)(2,1)S(1)}, u32[]{:S(2)}, u32[]{:S(2)}) collective-permute-start(bf16[128,2048]{1,0:T(8,128)(2,1)} %constant_dynamic-slice_fusion), channel_id=1, source_target_pairs={{0,2},{1,3},{2,0},{3,1},{4,6},{5,7},{6,4},{7,5},{8,10},{9,11},{10,... | collective-permute-start | bytes 1572872 | tf_op jit(solution)/shard_map/ppermute | solution.py:268
  12.0 14.7 %collective-permute-start.1 = (f32[2,128,128]{2,1,0:T(8,128)}, f32[2,128,128]{2,1,0:T(8,128)S(1)}, u32[]{:S(2)}, u32[]{:S(2)}) collective-permute-start(f32[2,128,128]{2,1,0:T(8,128)} %get-tuple-element.13), channel_id=1, source_target_pairs={{0,16},{8,24},{1,17},{9,25},{2,18},{10,26},{3,19},{11,27},{4,20},{... | collective-permute-start | bytes 393224 | tf_op jit(solution)/shard_map/ppermute | solution.py:373
  16.5 10.1 %collective-permute-start = (f32[2,128,128]{2,1,0:T(8,128)}, f32[2,128,128]{2,1,0:T(8,128)S(1)}, u32[]{:S(2)}, u32[]{:S(2)}) collective-permute-start(f32[2,128,128]{2,1,0:T(8,128)} %get-tuple-element.13), channel_id=1, source_target_pairs={{0,8},{8,16},{16,24},{1,9},{9,17},{17,25},{2,10},{10,18},{18,26},{... | collective-permute-start | bytes 393224 | tf_op jit(solution)/shard_map/ppermute | solution.py:373
  17.8 8.9 %copy-start.7 = (f32[2,128,128]{2,1,0:T(8,128)S(1)}, f32[2,128,128]{2,1,0:T(8,128)}, u32[]{:S(2)}) copy-start(f32[2,128,128]{2,1,0:T(8,128)} %param.11) | copy-start | bytes 393220
  32.1 30.7 %all-to-all-start.1 = ((bf16[8,256,256]{2,1,0:T(8,128)(2,1)}), bf16[8,256,256]{2,1,0:T(8,128)(2,1)S(1)}, u32[]{:S(2)}, u32[]{:S(2)}) async-start(bf16[8,256,256]{2,1,0:T(8,128)(2,1)} %attention_mix.1), calls=%async_computation.1 | async-start | bytes 2097152 | tf_op jit(solution)/shard_map/all_to_all | solution.py:413
  36.0 26.8 %collective-permute-start.9 = (bf16[128,2048]{1,0:T(8,128)(2,1)}, bf16[128,2048]{1,0:T(8,128)(2,1)}, u32[]{:S(2)}, u32[]{:S(2)}) collective-permute-start(bf16[128,2048]{1,0:T(8,128)(2,1)} %constant_dynamic-slice_fusion), channel_id=1, source_target_pairs={{0,6},{1,7},{2,4},{3,5},{4,2},{5,3},{6,0},{7,1},{8,14},{9,15},{10,... | collective-permute-start | bytes 1572872 | tf_op jit(solution)/shard_map/ppermute | solution.py:268
  38.9 3.2 %copy-start.5 = (bf16[128,2048]{1,0:T(8,128)(2,1)}, bf16[128,2048]{1,0:T(8,128)(2,1)S(1)}, u32[]{:S(2)}) copy-start(bf16[128,2048]{1,0:T(8,128)(2,1)S(1)} %collective-permute-done.3.rest_1_.refs_4_.refs_3_) | copy-start | bytes 1572868
  38.9 23.8 %collective-permute-start.8 = (bf16[128,2048]{1,0:T(8,128)(2,1)S(1)}, bf16[128,2048]{1,0:T(8,128)(2,1)}, u32[]{:S(2)}, u32[]{:S(2)}) collective-permute-start(bf16[128,2048]{1,0:T(8,128)(2,1)S(1)} %collective-permute-done.3.rest_1_.refs_4_.refs_3_), channel_id=1, source_target_pairs={{0,8},{8,0},{16,24},{24,16},{1,9},{9,1},{17,25},{25,17},{2,10},{10... | collective-permute-start | bytes 1572872 | tf_op jit(solution)/shard_map/ppermute | solution.py:268
  41.6 28.5 %collective-permute-start.4 = (bf16[128,2048]{1,0:T(8,128)(2,1)S(1)}, bf16[128,2048]{1,0:T(8,128)(2,1)S(1)}, u32[]{:S(2)}, u32[]{:S(2)}) collective-permute-start(bf16[128,2048]{1,0:T(8,128)(2,1)S(1)} %collective-permute-done.3.rest_1_.refs_4_.refs_3_), channel_id=1, source_target_pairs={{0,1},{1,0},{2,3},{3,2},{4,5},{5,4},{6,7},{7,6},{8,9},{9,8},{10,11... | collective-permute-start | bytes 1572872 | tf_op jit(solution)/shard_map/ppermute | solution.py:268
  41.6 28.5 %collective-permute-start.6 = (bf16[128,2048]{1,0:T(8,128)(2,1)}, bf16[128,2048]{1,0:T(8,128)(2,1)}, u32[]{:S(2)}, u32[]{:S(2)}) collective-permute-start(bf16[128,2048]{1,0:T(8,128)(2,1)} %collective-permute-done.5.rest_2_.refs_8_.refs_7_), channel_id=1, source_target_pairs={{0,1},{1,0},{2,3},{3,2},{4,5},{5,4},{6,7},{7,6},{8,9},{9,8},{10,11... | collective-permute-start | bytes 1572872 | tf_op jit(solution)/shard_map/ppermute | solution.py:268
  42.1 1.0 copy-start.3
  62.7 1.0 copy-start.4
  63.7 33.3 %all-to-all-start.2 = ((bf16[8,512,256]{2,1,0:T(8,128)(2,1)}), bf16[8,512,256]{2,1,0:T(8,128)(2,1)S(1)}, u32[]{:S(2)}, u32[]{:S(2)}) async-start(bf16[8,512,256]{2,1,0:T(8,128)(2,1)} %attention_both.3), calls=%async_computation.2 | async-start | bytes 4194304 | tf_op jit(solution)/shard_map/all_to_all | solution.py:413
  67.3 15.5 %collective-permute-start.10 = (bf16[128,2048]{1,0:T(8,128)(2,1)}, bf16[128,2048]{1,0:T(8,128)(2,1)}, u32[]{:S(2)}, u32[]{:S(2)}) collective-permute-start(bf16[128,2048]{1,0:T(8,128)(2,1)} %collective-permute-done.5.rest_2_.refs_8_.refs_7_), channel_id=1, source_target_pairs={{0,8},{8,0},{16,24},{24,16},{1,9},{9,1},{17,25},{25,17},{2,10},{10... | collective-permute-start | bytes 1572872 | tf_op jit(solution)/shard_map/ppermute | solution.py:268
  70.0 0.8 copy-start.6
  82.8 14.2 %collective-permute-start.13 = (bf16[128,2048]{1,0:T(8,128)(2,1)}, bf16[128,2048]{1,0:T(8,128)(2,1)}, u32[]{:S(2)}, u32[]{:S(2)}) collective-permute-start(bf16[128,2048]{1,0:T(8,128)(2,1)} %collective-permute-done.9.refs_12_.refs_11_), channel_id=1, source_target_pairs={{0,8},{8,0},{16,24},{24,16},{1,9},{9,1},{17,25},{25,17},{2,10},{10... | collective-permute-start | bytes 1572872 | tf_op jit(solution)/shard_map/ppermute | solution.py:268
  84.5 17.1 %collective-permute-start.14 = (bf16[128,2048]{1,0:T(8,128)(2,1)}, bf16[128,2048]{1,0:T(8,128)(2,1)}, u32[]{:S(2)}, u32[]{:S(2)}) collective-permute-start(bf16[128,2048]{1,0:T(8,128)(2,1)} %collective-permute-done.9.refs_12_.refs_11_), channel_id=1, source_target_pairs={{0,1},{1,0},{2,3},{3,2},{4,5},{5,4},{6,7},{7,6},{8,9},{9,8},{10,11... | collective-permute-start | bytes 1572872 | tf_op jit(solution)/shard_map/ppermute | solution.py:268
  84.5 17.1 %collective-permute-start.11 = (bf16[128,2048]{1,0:T(8,128)(2,1)}, bf16[128,2048]{1,0:T(8,128)(2,1)}, u32[]{:S(2)}, u32[]{:S(2)}) collective-permute-start(bf16[128,2048]{1,0:T(8,128)(2,1)} %collective-permute-done.8.refs_5_.refs_4_), channel_id=1, source_target_pairs={{0,1},{1,0},{2,3},{3,2},{4,5},{5,4},{6,7},{7,6},{8,9},{9,8},{10,11... | collective-permute-start | bytes 1572872 | tf_op jit(solution)/shard_map/ppermute | solution.py:268
  85.0 16.6 %collective-permute-start.12 = (bf16[128,2048]{1,0:T(8,128)(2,1)}, bf16[128,2048]{1,0:T(8,128)(2,1)}, u32[]{:S(2)}, u32[]{:S(2)}) collective-permute-start(bf16[128,2048]{1,0:T(8,128)(2,1)} %collective-permute-done.10.refs_9_.refs_8_), channel_id=1, source_target_pairs={{0,1},{1,0},{2,3},{3,2},{4,5},{5,4},{6,7},{7,6},{8,9},{9,8},{10,11... | collective-permute-start | bytes 1572872 | tf_op jit(solution)/shard_map/ppermute | solution.py:268
  97.0 4.6 %collective-permute-start.15 = (bf16[128,2048]{1,0:T(8,128)(2,1)}, bf16[128,2048]{1,0:T(8,128)(2,1)}, u32[]{:S(2)}, u32[]{:S(2)}) collective-permute-start(bf16[128,2048]{1,0:T(8,128)(2,1)} %collective-permute-done.13.refs_13_.refs_12_), channel_id=1, source_target_pairs={{0,1},{1,0},{2,3},{3,2},{4,5},{5,4},{6,7},{7,6},{8,9},{9,8},{10,11... | collective-permute-start | bytes 1572872 | tf_op jit(solution)/shard_map/ppermute | solution.py:268
  97.0 4.7 %copy-start.2 = (bf16[8,512,256]{2,1,0:T(8,128)(2,1)}, bf16[8,512,256]{2,1,0:T(8,128)(2,1)S(1)}, u32[]{:S(2)}) copy-start(bf16[8,512,256]{2,1,0:T(8,128)(2,1)S(1)} %all-to-all-done.2.refs_1_) | copy-start | bytes 6291460
  97.0 19.4 %all-to-all-start = ((bf16[8,256,256]{2,1,0:T(8,128)(2,1)}), bf16[8,256,256]{2,1,0:T(8,128)(2,1)S(1)}, u32[]{:S(2)}, u32[]{:S(2)}) async-start(bf16[8,256,256]{2,1,0:T(8,128)(2,1)} %attention_both.2), calls=%async_computation | async-start | bytes 2097152 | tf_op jit(solution)/shard_map/all_to_all | solution.py:413
  116.4 1.0 copy-start
where the time goes:
time: 127 us; the launch traced here: 125 us
  Pallas kernels  67.4 us (53%)
  starting transfers between devices  29.5 us (23%)
  waiting for transfers between devices  21 us (17%)
  local copies, waits for them, and re-layouts  4.64 us (4%)
  other arithmetic  1.38 us (1%)
    pallas_call x4, Pallas kernels, chunk_call(): call(functools.partial(body, blocks, per_dest), f'attention_{kind}', jax....  42.4 us
    pallas_call x2, Pallas kernels, project(): pl.pallas_call(functools.partial(project_body, count=len(chunks), parts_o...  18.9 us
    ppermute x13, waiting for transfers between devices, flip(): return lax.ppermute(array, axis, [(at, at ^ turn) for at in range(size)])  14.6 us
    ppermute x13, starting transfers between devices, flip(): return lax.ppermute(array, axis, [(at, at ^ turn) for at in range(size)])  14.1 us
    all_to_all x3, starting transfers between devices, per_device(): lax.all_to_all(chunk, 'head', split_axis=0, concat_axis=0, tiled=True)  11.5 us
    pallas_call x1, Pallas kernels, kv_terms(): call(kv_body, 'kv_terms', (jax.ShapeDtypeStruct((segs, heads, HD, HD), F3...  6.08 us
    ppermute x3, starting transfers between devices, per_device(): lax.ppermute(total, 'seq', [(at, at + step) for at in range(seq_size - st...  3.84 us
    unnamed x16, local copies, waits for them, and re-layouts  3.8 us
  transfers between devices with their start and end apart: 19, of which 5 were waited for; matrix products, arithmetic and copies ran while one was open for 2% of the time, Pallas kernels for 48%

commit v1 on v0

v1 whole, which is shorter than its diff:
```python
import functools

import jax
import jax.numpy as jnp
from jax import lax
from jax.experimental import pallas as pl
from jax.experimental.pallas import tpu as pltpu
from jax.sharding import PartitionSpec as P

HD = 128
SEG = 2048
BLOCK = 256
EPS = 1e-06
LOG2E = 1.4426950408889634
VMEM = 60 << 20
PROJECT_VMEM = 44 << 20
F32, BF16 = jnp.float32, jnp.bfloat16


def call(body, name, out_shape, grid_spec, flops, bytes_accessed, transcendentals=0):
    return pl.pallas_call(
        body,
        name=name,
        out_shape=out_shape,
        grid_spec=grid_spec,
        compiler_params=pltpu.CompilerParams(vmem_limit_bytes=VMEM),
        cost_estimate=pl.CostEstimate(
            flops=flops, bytes_accessed=bytes_accessed, transcendentals=transcendentals
        ),
    )


def whole(shape, memory_space=pltpu.VMEM):
    return pl.BlockSpec(shape, lambda *_: (0,) * len(shape), memory_space=memory_space)


def elu_feature(source):
    wide = source.astype(F32)
    return jnp.where(wide > 0, wide + 1.0, jnp.exp(wide)).astype(BF16)


def columns(head):
    return slice(head * HD, (head + 1) * HD)


def kv_body(k_ref, v_ref, term_ref, total_ref, held):
    for head in range(k_ref.shape[1] // HD):
        cols = columns(head)
        term = lax.dot_general(
            elu_feature(k_ref[:, cols]),
            v_ref[:, cols],
            (((0,), (0,)), ((), ())),
            preferred_element_type=F32,
        )
        term_ref[0, head] = term

        total = jnp.where(pl.program_id(0) == 0, 0.0, held[head]) + term
        held[head] = total
        total_ref[head] = total.astype(BF16)


def kv_terms(keys, values):
    tokens, width = keys.shape
    heads, segs = width // HD, tokens // SEG
    block = pl.BlockSpec((SEG, width), lambda seg: (seg, 0))
    return call(
        kv_body,
        "kv_terms",
        (
            jax.ShapeDtypeStruct((segs, heads, HD, HD), F32),
            jax.ShapeDtypeStruct((heads, HD, HD), BF16),
        ),
        pl.GridSpec(
            grid=(segs,),
            in_specs=[block, block],
            out_specs=[
                pl.BlockSpec((1, heads, HD, HD), lambda seg: (seg, 0, 0, 0)),
                whole((heads, HD, HD)),
            ],
            scratch_shapes=[pltpu.VMEM((heads, HD, HD), F32)],
        ),
        2 * tokens * width * HD,
        2 * keys.size * 2,
    )(keys, values)


def mean_square(source):
    return jnp.mean(source * source, axis=-1, keepdims=True)


def scores_of(q, k):
    rows, end = q.shape[0], k.shape[0]
    wide = q.astype(F32) * (HD**-0.5 * LOG2E)
    high = wide.astype(BF16)
    low = (wide - high.astype(F32)).astype(BF16)
    scores = lax.dot_general(
        jnp.concatenate([high, low], axis=1),
        jnp.concatenate([k, k], axis=1),
        (((1,), (1,)), ((), ())),
        preferred_element_type=F32,
    )
    row = lax.broadcasted_iota(jnp.int32, (rows, rows), 0)
    col = lax.broadcasted_iota(jnp.int32, (rows, rows), 1)
    diagonal = jnp.where(col <= row, scores[:, end - rows :], -jnp.inf)
    if end > rows:
        return jnp.concatenate([scores[:, : end - rows], diagonal], axis=1)
    return diagonal


def local_branch(scores, v, scale_gain):
    largest = jnp.max(scores, axis=-1, keepdims=True)
    weights = jnp.exp2(scores - largest).astype(BF16)
    summed = jnp.dot(
        weights, jnp.concatenate([v, jnp.ones_like(v)], axis=1), preferred_element_type=F32
    )
    local, denominator = summed[:, :HD], summed[:, HD:]
    return local * (
        lax.rsqrt(mean_square(local) + EPS * denominator * denominator) * scale_gain
    )


def score_ahead(units, q_ref, k_ref, use):
    def make(unit):
        dest, rows, end, head = unit
        return scores_of(q_ref[0, dest, rows, columns(head)], k_ref[:end, columns(head)])

    ahead = make(units[0])
    for unit, following in zip(units, [*units[1:], None]):
        scores = ahead
        if following is not None:
            ahead = make(following)
        use(unit, scores)


def memory_branch(q, memory_pair, scale_gain):
    both = jnp.dot(elu_feature(q), memory_pair, preferred_element_type=F32)
    read = both[:, :HD] + both[:, HD:]
    return read * (lax.rsqrt(mean_square(read) + EPS) * scale_gain)


def gate_of(beta_ref, head):
    return 1.0 / (1.0 + jnp.exp(-jnp.full((1, HD), beta_ref[head], F32)))


def units_of(dests, per_dest, block, heads):
    start, size = block
    step = BLOCK if size % BLOCK == 0 else size
    return [
        (dest, slice(at, at + step), dest * per_dest + start + at + step, head)
        for dest in range(dests)
        for at in range(0, size, step)
        for head in range(heads)
    ]


def memory_pairs(init_ref, total_refs, term_ref, memory, prefix_ref, prefix_scale):
    @pl.when(pl.program_id(0) == 0)
    def _():
        for head in range(memory.shape[0]):
            now = init_ref[head]
            for total_ref in total_refs:
                now = now + total_ref[head].astype(F32)
            memory[head] = now
            prefix_ref[0, head] = now * prefix_scale

    pairs = []
    for head in range(memory.shape[0]):
        now = memory[head]
        high = now.astype(BF16)
        low = (now - high.astype(F32)).astype(BF16)
        pairs.append(jnp.concatenate([high, low], axis=1))
        memory[head] = now + term_ref[0, head]
    return pairs


def chunk_body(
    block,
    per_dest,
    prefix_scale,
    earlier,
    q_ref,
    k_ref,
    v_ref,
    init_ref,
    term_ref,
    beta_ref,
    mem_gain_ref,
    loc_gain_ref,
    *rest,
):
    *_, out_ref, prefix_ref, memory = rest
    _, dests, _, width = q_ref.shape
    pairs = memory_pairs(
        init_ref, rest[:earlier], term_ref, memory, prefix_ref, prefix_scale
    )

    def use(unit, scores):
        dest, rows, end, head = unit
        cols = columns(head)
        gate = gate_of(beta_ref, head)
        local = local_branch(scores, v_ref[:end, cols], (1.0 - gate) * loc_gain_ref[:, cols])
        read = memory_branch(q_ref[0, dest, rows, cols], pairs[head], gate * mem_gain_ref[:, cols])
        out_ref[dest, rows, cols] = (read + local).astype(BF16)

    score_ahead(units_of(dests, per_dest, block, width // HD), q_ref, k_ref, use)


def chunk_call(block, dests, arrays, totals, after, cost=1):
    query, keys, values, init, terms, beta, mem_gain, loc_gain = arrays
    tokens, width = query.shape
    segs, heads = tokens // SEG, width // HD
    per_dest = SEG // dests
    start, size = block
    q = query.reshape(segs, dests, per_dest, width)
    q_block = tuple(map(pl.Element, (1, dests, size, width)))
    segment = pl.BlockSpec((SEG, width), lambda seg: (seg, 0))
    prefix_shape = (1, heads, HD, HD)
    pairs_met = segs * heads * size * sum(dest * per_dest + start + size for dest in range(dests))
    return call(
        functools.partial(chunk_body, block, per_dest, tokens**-0.5, len(totals)),
        "attention",
        [
            jax.ShapeDtypeStruct((segs * dests, size, width), BF16),
            jax.ShapeDtypeStruct(prefix_shape, F32),
        ],
        pl.GridSpec(
            grid=(segs,),
            in_specs=[
                pl.BlockSpec(q_block, lambda seg: (seg, 0, start, 0)),
                segment,
                segment,
                whole(init.shape),
                pl.BlockSpec((1, heads, HD, HD), lambda seg: (seg, 0, 0, 0)),
                pl.BlockSpec(memory_space=pltpu.SMEM),
                whole(mem_gain.shape),
                whole(loc_gain.shape),
                *[whole(init.shape)] * len(totals),
                *[pl.BlockSpec(memory_space=pl.ANY)] * len(after),
            ],
            out_specs=[
                pl.BlockSpec((dests, size, width), lambda seg: (seg, 0, 0)),
                whole(prefix_shape),
            ],
            scratch_shapes=[pltpu.VMEM((heads, HD, HD), F32)],
        ),
        int(cost * 8 * pairs_met * HD),
        int(cost * 6 * tokens * width),
        int(cost * pairs_met),
    )(q, *arrays[1:], *totals, *after)


def flip(array, axis, size, turn):
    return lax.ppermute(array, axis, [(at, at ^ turn) for at in range(size)])


class RowGather:
    def __init__(self, w_out, seq_size, head_size):
        half = w_out.shape[0] // 2
        self.seq_size, self.head_size = seq_size, head_size
        self.paired = seq_size % 2 == 0 and half % HD == 0
        own = w_out
        if self.paired:
            own = lax.dynamic_slice_in_dim(w_out, lax.axis_index("seq") % 2 * half, half, 0)
        self.pieces = {0: [w_out]}
        self.own = own

    def near(self):
        for turn in range(2, self.head_size, 2):
            self.pieces[turn] = [flip(self.own, "head", self.head_size, turn)]

    def swap(self, turn):
        if self.paired:
            self.pieces[turn].append(flip(self.pieces[turn][0], "seq", self.seq_size, 1))

    def across(self, turn):
        done = self.pieces.setdefault(turn + 1, [])
        for piece in self.pieces[turn][len(done) :]:
            done.append(flip(piece, "head", self.head_size, 1))

    def now(self, *turns):
        return [piece for turn in turns for piece in self.pieces[turn]]

    def all(self):
        return [tuple(self.pieces[turn]) for turn in range(self.head_size)]


def project_body(place_ref, *refs, parts_of, first, groups):
    row_ref, w_refs = refs[0], refs[1 : 1 + sum(parts_of)]
    out_ref, row_held, total, out_held, w_held, sems = refs[-6:]
    count, out_width = out_held.shape
    width = row_ref.shape[2]
    row_copy = pltpu.make_async_copy(row_ref, row_held, sems.at[len(w_refs)])
    row_copy.start()
    copies, places = [], []
    for turn, parts in enumerate(parts_of):
        source, size = place_ref[0] ^ turn, width // parts
        for part in range(parts):
            at, row = len(copies), turn * width + part * size
            copies.append(pltpu.make_async_copy(w_refs[at], w_held.at[row : row + size], sems.at[at]))
            copies[-1].start()
            place = part if parts == 1 else place_ref[1] ^ part
            places.append((turn, source, pl.ds(pl.multiple_of(place * size, size), size)))
    row_copy.wait()
    step = len(parts_of) // groups
    strip = out_width // groups
    sends = []
    for group in range(groups):
        found = []
        for copy, (turn, source, cols) in zip(copies, places):
            if turn // step == group:
                copy.wait()
                found.append(row_held[source, :, cols])
        rows = jnp.concatenate(found, axis=1)
        met = slice(group * step * width, (group + 1) * step * width)
        for at in range(groups):
            cols = slice(at * strip, (at + 1) * strip)
            term = jnp.dot(rows, w_held[met, cols], preferred_element_type=F32)
            if group > 0:
                term = total[:, cols] + term
            if group < groups - 1:
                total[:, cols] = term
            else:
                out_held[:, cols] = term.astype(BF16)
                sends.append(
                    pltpu.make_async_copy(
                        out_held.at[:, cols],
                        out_ref.at[first : first + count, cols],
                        sems.at[len(w_refs) + 1 + at],
                    )
                )
                sends[-1].start()
    for send in sends:
        send.wait()


def project(place, chunk, pieces, first, tokens, so_far=None):
    sources, count, width = chunk.shape
    flat = [part for piece in pieces for part in piece]
    depth, out_width = width * sources, flat[0].shape[1]
    groups = 4 if sources % 4 == 0 and out_width % 512 == 0 else 1
    extra = () if so_far is None else (so_far,)
    operands = (chunk, *flat, *extra)
    anywhere = pl.BlockSpec(memory_space=pl.ANY)
    return pl.pallas_call(
        functools.partial(
            project_body, parts_of=tuple(map(len, pieces)), first=first, groups=groups
        ),
        name="project",
        out_shape=jax.ShapeDtypeStruct((tokens, out_width), BF16),
        grid_spec=pltpu.PrefetchScalarGridSpec(
            num_scalar_prefetch=1,
            grid=(1,),
            in_specs=[anywhere] * len(operands),
            out_specs=anywhere,
            scratch_shapes=[
                pltpu.VMEM(chunk.shape, BF16),
                pltpu.VMEM((count, out_width), F32),
                pltpu.VMEM((count, out_width), BF16),
                pltpu.VMEM((depth, out_width), BF16),
                pltpu.SemaphoreType.DMA((len(flat) + 1 + groups,)),
            ],
        ),
        input_output_aliases={} if so_far is None else {len(operands): 0},
        compiler_params=pltpu.CompilerParams(vmem_limit_bytes=PROJECT_VMEM),
        cost_estimate=pl.CostEstimate(
            flops=2 * count * depth * out_width,
            bytes_accessed=2 * (count * depth + depth * out_width + count * out_width),
            transcendentals=0,
        ),
    )(place, *operands)


def per_device(
    sizes, query, keys, values, mem_init, beta, mem_gain, loc_gain, w_out
):
    seq_size, head_size = sizes
    tokens, width = query.shape
    dests = head_size * SEG // tokens
    per_dest = SEG // dests
    me, now = lax.axis_index("head"), lax.axis_index("seq")
    place = jnp.stack([me, now % 2]).astype(jnp.int32)
    mem_gain, loc_gain = mem_gain.reshape(1, width), loc_gain.reshape(1, width)

    gather = RowGather(w_out, seq_size, head_size)
    gather.near()
    terms, total = kv_terms(keys, values)
    totals = [
        lax.ppermute(total, "seq", [(at, at + step) for at in range(seq_size - step)])
        for step in range(1, seq_size)
    ]

    groups = [(0, per_dest // 2), (per_dest // 2, per_dest // 2)]
    *near, last = range(2, head_size, 2)
    arrays = (query, keys, values, mem_init, terms, beta, mem_gain, loc_gain)
    arrived, after = [], ()
    for block in groups:
        first = block == groups[0]
        chunk, prefix = chunk_call(block, dests, arrays, totals, after, 0.01 if first else 20)
        if first:
            memory_prefix = prefix
            after = gather.now(*near, last)
        else:
            for turn in near:
                gather.swap(turn)
            chunk, early = lax.optimization_barrier((chunk, [gather.pieces[turn] for turn in near]))
            gather.pieces.update(zip(near, early))
            _, held = lax.optimization_barrier((chunk, gather.pieces[last]))
            gather.pieces[last] = held
            gather.swap(last)
            for turn in (0, *near, last):
                gather.across(turn)
        arrived.append(lax.all_to_all(chunk, "head", split_axis=0, concat_axis=0, tiled=True))
    pieces = gather.all()
    out = None
    for (start, _), chunk in zip(groups, arrived):
        out = project(place, chunk, pieces, start, tokens // head_size, out)
    return out, memory_prefix


def solution(mesh):
    sizes = (mesh.shape["seq"], mesh.shape["head"])
    in_specs = (
        P("seq", "head"),
        P("seq", "head"),
        P("seq", "head"),
        P("head", None, None),
        P("head"),
        P("head"),
        P("head"),
        P("head", None),
    )
    out_specs = (P(("seq", "head"), None), P("seq", "head", None, None))
    return jax.shard_map(
        functools.partial(per_device, sizes),
        mesh=mesh,
        in_specs=in_specs,
        out_specs=out_specs,
        check_vma=False,
    )
```

time: 127 us -> 113 us (0.89); the launches traced: 125 us -> 112 us
  waiting for transfers between devices: 21 us -> 31.2 us
  starting transfers between devices: 29.5 us -> 19.7 us
  Pallas kernels: 67.4 us -> 58 us
  local copies, waits for them, and re-layouts: 4.64 us -> 2.5 us
  other arithmetic: 1.38 us -> 0.07 us
    pallas_call x6 -> x4, Pallas kernels: 61.4 us -> 52 us  [the longest x2 34.5 us: chunk_call(): call(functools.partial(chunk_body, block, per_dest, tokens ** (-0.5), len...]
    ppermute x3, waiting for transfers between devices: 3.27 us -> 10.8 us  [per_device(): lax.ppermute(total, 'seq', [(at, at + step) for at in range(seq_size - st...]
    ppermute x13, starting transfers between devices: 14.1 us -> 7.03 us  [flip(): return lax.ppermute(array, axis, [(at, at ^ turn) for at in range(size)])]
    ppermute x13, waiting for transfers between devices: 14.6 us -> 18.3 us  [flip(): return lax.ppermute(array, axis, [(at, at ^ turn) for at in range(size)])]
    all_to_all x3 -> x2, starting transfers between devices: 11.5 us -> 8.86 us  [per_device(): lax.all_to_all(chunk, 'head', split_axis=0, concat_axis=0, tiled=True)]
    unnamed x16 -> x10, local copies, waits for them, and re-layouts: 3.8 us -> 1.42 us
    all_to_all x3 -> x2, waiting for transfers between devices: 3.16 us -> 2.15 us  [per_device(): lax.all_to_all(chunk, 'head', split_axis=0, concat_axis=0, tiled=True)]
  transfers between devices with their start and end apart: 19 -> 18, of which waited for: 5 -> 9; matrix products, arithmetic and copies ran while one was open for 2% -> 0% of each run, Pallas kernels for 48% -> 44%
where the time goes in v1:
time: 113 us; the launch traced here: 112 us
  Pallas kernels  58 us (51%)
  waiting for transfers between devices  31.2 us (28%)
  starting transfers between devices  19.7 us (17%)
  local copies, waits for them, and re-layouts  2.5 us (2%)
    pallas_call x2, Pallas kernels, chunk_call(): call(functools.partial(chunk_body, block, per_dest, tokens ** (-0.5), len...  34.5 us
    ppermute x13, waiting for transfers between devices, flip(): return lax.ppermute(array, axis, [(at, at ^ turn) for at in range(size)])  18.3 us
    pallas_call x2, Pallas kernels, project(): pl.pallas_call(functools.partial(project_body, parts_of=tuple(map(len, pi...  17.5 us
    ppermute x3, waiting for transfers between devices, per_device(): lax.ppermute(total, 'seq', [(at, at + step) for at in range(seq_size - st...  10.8 us
    all_to_all x2, starting transfers between devices, per_device(): lax.all_to_all(chunk, 'head', split_axis=0, concat_axis=0, tiled=True)  8.86 us
    ppermute x13, starting transfers between devices, flip(): return lax.ppermute(array, axis, [(at, at ^ turn) for at in range(size)])  7.03 us
    pallas_call x1, Pallas kernels, kv_terms(): call(kv_body, 'kv_terms', (jax.ShapeDtypeStruct((segs, heads, HD, HD), F3...  5.97 us
    ppermute x3, starting transfers between devices, per_device(): lax.ppermute(total, 'seq', [(at, at + step) for at in range(seq_size - st...  3.85 us
  transfers between devices with their start and end apart: 18, of which 9 were waited for; matrix products, arithmetic and copies ran while one was open for 0% of the time, Pallas kernels for 44%

profile of v1, /device:TPU:24, one launch (start us, length us, event | category | flops | bytes accessed | tf_op | source)
XLA Modules:
  0.0 112.5 jit_solution(4040375047028893462)
XLA Ops:
  0.6 1.1 constant_dynamic-slice_fusion
  1.7 1.6 %collective-permute-start.4 = (bf16[128,2048]{1,0:T(8,128)(2,1)S(1)}, bf16[128,2048]{1,0:T(8,128)(2,1)}, u32[]{:S(2)}, u32[]{:S(2)}) collective-permute-start(bf16[128,2048]{1,0:T(8,128)(2,1)S(1)} %constant_dynamic-slice_fusion), channel_id=1, source_target_pairs={{0,4},{1,5},{2,6},{3,7},{4,0},{5,1},{6,2},{7,3},{8,12},{9,13},{10,... | collective-permute-start | bytes 1572872 | tf_op jit(solution)/shard_map/ppermute | solution.py:253
  3.3 1.5 %collective-permute-start.3 = (bf16[128,2048]{1,0:T(8,128)(2,1)S(1)}, bf16[128,2048]{1,0:T(8,128)(2,1)}, u32[]{:S(2)}, u32[]{:S(2)}) collective-permute-start(bf16[128,2048]{1,0:T(8,128)(2,1)S(1)} %constant_dynamic-slice_fusion), channel_id=1, source_target_pairs={{0,2},{1,3},{2,0},{3,1},{4,6},{5,7},{6,4},{7,5},{8,10},{9,11},{10,... | collective-permute-start | bytes 1572872 | tf_op jit(solution)/shard_map/ppermute | solution.py:253
  4.8 0.5 collective-permute-start.5
  5.3 6.0 %kv_terms.1 = (f32[4,2,128,128]{3,2,1,0:T(8,128)}, bf16[2,128,128]{2,1,0:T(8,128)(2,1)}) custom-call(bf16[8192,256]{1,0:T(8,128)(2,1)} %k_ref.5, bf16[8192,256]{1,0:T(8,128)(2,1)} %v_ref.5), custom_call_target="tpu_custom_call" | custom-call | flops 536870912 | bytes 8388608 | tf_op jit(solution)/shard_map/kv_terms/pallas_call | solution.py:66
  11.3 1.3 %collective-permute-start.2 = (bf16[2,128,128]{2,1,0:T(8,128)(2,1)}, bf16[2,128,128]{2,1,0:T(8,128)(2,1)S(1)}, u32[]{:S(2)}, u32[]{:S(2)}) collective-permute-start(bf16[2,128,128]{2,1,0:T(8,128)(2,1)} %get-tuple-element.14), channel_id=1, source_target_pairs={{0,24},{1,25},{2,26},{3,27},{4,28},{5,29},{6,30},{7,31}} | collective-permute-start | bytes 196616 | tf_op jit(solution)/shard_map/ppermute | solution.py:388
  12.5 1.3 %collective-permute-start.1 = (bf16[2,128,128]{2,1,0:T(8,128)(2,1)}, bf16[2,128,128]{2,1,0:T(8,128)(2,1)S(1)}, u32[]{:S(2)}, u32[]{:S(2)}) collective-permute-start(bf16[2,128,128]{2,1,0:T(8,128)(2,1)} %get-tuple-element.14), channel_id=1, source_target_pairs={{0,16},{8,24},{1,17},{9,25},{2,18},{10,26},{3,19},{11,27},{4,20},{... | collective-permute-start | bytes 196616 | tf_op jit(solution)/shard_map/ppermute | solution.py:388
  13.8 5.7 %collective-permute-done.2.rest_2_ = bf16[2,128,128]{2,1,0:T(8,128)(2,1)S(1)} collective-permute-done((bf16[2,128,128]{2,1,0:T(8,128)(2,1)}, bf16[2,128,128]{2,1,0:T(8,128)(2,1)S(1)}, u32[]{:S(2)}, u32[]{:S(2)}) %collective-permute-start.2) | collective-permute-done | bytes 65568 | tf_op jit(solution)/shard_map/ppermute | solution.py:388
  19.5 1.3 %collective-permute-start = (bf16[2,128,128]{2,1,0:T(8,128)(2,1)}, bf16[2,128,128]{2,1,0:T(8,128)(2,1)S(1)}, u32[]{:S(2)}, u32[]{:S(2)}) collective-permute-start(bf16[2,128,128]{2,1,0:T(8,128)(2,1)} %get-tuple-element.14), channel_id=1, source_target_pairs={{0,8},{8,16},{16,24},{1,9},{9,17},{17,25},{2,10},{10,18},{18,26},{... | collective-permute-start | bytes 196616 | tf_op jit(solution)/shard_map/ppermute | solution.py:388
  20.8 0.8 collective-permute-done.1.rest_1_
  21.7 4.3 %collective-permute-done.rest_0_ = bf16[2,128,128]{2,1,0:T(8,128)(2,1)S(1)} collective-permute-done((bf16[2,128,128]{2,1,0:T(8,128)(2,1)}, bf16[2,128,128]{2,1,0:T(8,128)(2,1)S(1)}, u32[]{:S(2)}, u32[]{:S(2)}) %collective-permute-start) | collective-permute-done | bytes 65568 | tf_op jit(solution)/shard_map/ppermute | solution.py:388
  25.9 0.6 copy-done.4
  26.5 15.0 %attention.3 = (bf16[8,512,256]{2,1,0:T(8,128)(2,1)}, f32[1,2,128,128]{3,2,1,0:T(8,128)}) custom-call(bf16[4,2,1024,256]{3,2,1,0:T(8,128)(2,1)} %bitcast.5, bf16[8192,256]{1,0:T(8,128)(2,1)} %k_ref.5, bf16[8192,256]{1,0:T(8,128)(2,1)} %v_ref.5, f32[2,128,128]{2,1,0:T(8,128)} %init_ref.3, f32[4,2,128,128]{3,2,1,0:T(8,128)} %get-tuple-element.13.term_ref, ...), custom_call_target="tpu_custom_call" | custom-call | flops 85899344 | bytes 125829 | tf_op jit(solution)/shard_map/attention/pallas_call | solution.py:219
  41.6 4.3 %all-to-all-start.1 = ((bf16[8,512,256]{2,1,0:T(8,128)(2,1)}), bf16[8,512,256]{2,1,0:T(8,128)(2,1)}, u32[]{:S(2)}, u32[]{:S(2)}) async-start(bf16[8,512,256]{2,1,0:T(8,128)(2,1)} %get-tuple-element.22), calls=%async_computation.1 | async-start | bytes 4194304 | tf_op jit(solution)/shard_map/all_to_all | solution.py:412
  46.0 2.0 %collective-permute-start.6 = (bf16[128,2048]{1,0:T(8,128)(2,1)}, bf16[128,2048]{1,0:T(8,128)(2,1)}, u32[]{:S(2)}, u32[]{:S(2)}) collective-permute-start(bf16[128,2048]{1,0:T(8,128)(2,1)} %collective-permute-done.3.rest_3_.refs_3_), channel_id=1, source_target_pairs={{0,8},{8,0},{16,24},{24,16},{1,9},{9,1},{17,25},{25,17},{2,10},{10... | collective-permute-start | bytes 1572872 | tf_op jit(solution)/shard_map/ppermute | solution.py:253
  48.0 0.8 copy-done
  48.8 19.5 %attention.2 = (bf16[8,512,256]{2,1,0:T(8,128)(2,1)}, f32[1,2,128,128]{3,2,1,0:T(8,128)}) custom-call(bf16[4,2,1024,256]{3,2,1,0:T(8,128)(2,1)} %bitcast.6, bf16[8192,256]{1,0:T(8,128)(2,1)} %k_ref.5, bf16[8192,256]{1,0:T(8,128)(2,1)} %v_ref.5, f32[2,128,128]{2,1,0:T(8,128)} %init_ref.3, f32[4,2,128,128]{3,2,1,0:T(8,128)} %get-tuple-element.13.term_ref, ...), custom_call_target="tpu_custom_call" | custom-call | flops 257698037760 | bytes 251658240 | tf_op jit(solution)/shard_map/attention/pallas_call | solution.py:219
  68.4 3.3 %collective-permute-done.6.refs_4_ = bf16[128,2048]{1,0:T(8,128)(2,1)} collective-permute-done((bf16[128,2048]{1,0:T(8,128)(2,1)}, bf16[128,2048]{1,0:T(8,128)(2,1)}, u32[]{:S(2)}, u32[]{:S(2)}) %collective-permute-start.6) | collective-permute-done | bytes 524320 | tf_op jit(solution)/shard_map/ppermute | solution.py:253
  71.7 0.9 all-to-all-done.1.refs_0_
  72.6 4.5 %all-to-all-start = ((bf16[8,512,256]{2,1,0:T(8,128)(2,1)}), bf16[8,512,256]{2,1,0:T(8,128)(2,1)}, u32[]{:S(2)}, u32[]{:S(2)}) async-start(bf16[8,512,256]{2,1,0:T(8,128)(2,1)} %get-tuple-element.16), calls=%async_computation | async-start | bytes 4194304 | tf_op jit(solution)/shard_map/all_to_all | solution.py:412
  77.1 0.2 collective-permute-start.14
  77.3 0.4 collective-permute-start.9
  77.7 0.2 collective-permute-start.10
  77.8 0.4 collective-permute-start.11
  78.2 0.9 collective-permute-done.14.refs_13_
  79.1 0.3 collective-permute-start.12
  79.3 12.1 %collective-permute-done.13.refs_12_ = bf16[128,2048]{1,0:T(8,128)(2,1)S(1)} collective-permute-done((bf16[128,2048]{1,0:T(8,128)(2,1)S(1)}, bf16[128,2048]{1,0:T(8,128)(2,1)S(1)}, u32[]{:S(2)}, u32[]{:S(2)}) %collective-permute-start.13) | collective-permute-done | bytes 524320 | tf_op jit(solution)/shard_map/ppermute | solution.py:253
  91.5 0.1 pad_add_fusion.place_ref
  91.6 1.9 %collective-permute-done.15.refs_14_ = bf16[128,2048]{1,0:T(8,128)(2,1)} collective-permute-done((bf16[128,2048]{1,0:T(8,128)(2,1)S(1)}, bf16[128,2048]{1,0:T(8,128)(2,1)}, u32[]{:S(2)}, u32[]{:S(2)}) %collective-permute-start.15) | collective-permute-done | bytes 524320 | tf_op jit(solution)/shard_map/ppermute | solution.py:253
  93.5 8.7 %project.2.refs_15_ = bf16[1024,2048]{1,0:T(8,128)(2,1)} custom-call(s32[2]{0:T(128)S(1)} %pad_add_fusion.place_ref, bf16[8,512,256]{2,1,0:T(8,128)(2,1)} %all-to-all-done.1.refs_0_, bf16[256,2048]{1,0:T(8,128)(2,1)} %refs_1_.3, bf16[256,2048]{1,0:T(8,128)(2,1)} %collective-permute-done.8.refs_2_, bf16[128,2048]{1,0:T(8,128)(2,1)} %collective-permute-done.3.rest_3_.refs_3_, ...), custom_call_target="tpu_custom_call" | custom-call | flops 4294967296 | bytes 12582912 | tf_op jit(solution)/shard_map/project/pallas_call | solution.py:344
  102.3 1.3 %all-to-all-done.refs_0_ = bf16[8,512,256]{2,1,0:T(8,128)(2,1)} async-done(((bf16[8,512,256]{2,1,0:T(8,128)(2,1)}), bf16[8,512,256]{2,1,0:T(8,128)(2,1)}, u32[]{:S(2)}, u32[]{:S(2)}) %all-to-all-start) | async-done | bytes 2097184 | tf_op jit(solution)/shard_map/all_to_all | solution.py:412
  103.6 8.8 %project.3 = bf16[1024,2048]{1,0:T(8,128)(2,1)} custom-call(s32[2]{0:T(128)S(1)} %pad_add_fusion.place_ref, bf16[8,512,256]{2,1,0:T(8,128)(2,1)} %all-to-all-done.refs_0_, bf16[256,2048]{1,0:T(8,128)(2,1)} %refs_1_.3, bf16[256,2048]{1,0:T(8,128)(2,1)} %collective-permute-done.8.refs_2_, ...), custom_call_target="tpu_custom_call", output_to_operand_aliasing={{}: (16, {})} | custom-call | flops 4294967296 | bytes 12582912 | tf_op jit(solution)/shard_map/project/pallas_call | solution.py:344
  (21 shorter events, 0.1 us)
Async XLA Ops:
  1.7 44.2 %collective-permute-start.4 = (bf16[128,2048]{1,0:T(8,128)(2,1)S(1)}, bf16[128,2048]{1,0:T(8,128)(2,1)}, u32[]{:S(2)}, u32[]{:S(2)}) collective-permute-start(bf16[128,2048]{1,0:T(8,128)(2,1)S(1)} %constant_dynamic-slice_fusion), channel_id=1, source_target_pairs={{0,4},{1,5},{2,6},{3,7},{4,0},{5,1},{6,2},{7,3},{8,12},{9,13},{10,... | collective-permute-start | bytes 1572872 | tf_op jit(solution)/shard_map/ppermute | solution.py:253
  3.3 42.7 %collective-permute-start.3 = (bf16[128,2048]{1,0:T(8,128)(2,1)S(1)}, bf16[128,2048]{1,0:T(8,128)(2,1)}, u32[]{:S(2)}, u32[]{:S(2)}) collective-permute-start(bf16[128,2048]{1,0:T(8,128)(2,1)S(1)} %constant_dynamic-slice_fusion), channel_id=1, source_target_pairs={{0,2},{1,3},{2,0},{3,1},{4,6},{5,7},{6,4},{7,5},{8,10},{9,11},{10,... | collective-permute-start | bytes 1572872 | tf_op jit(solution)/shard_map/ppermute | solution.py:253
  4.8 43.2 %collective-permute-start.5 = (bf16[128,2048]{1,0:T(8,128)(2,1)S(1)}, bf16[128,2048]{1,0:T(8,128)(2,1)S(1)}, u32[]{:S(2)}, u32[]{:S(2)}) collective-permute-start(bf16[128,2048]{1,0:T(8,128)(2,1)S(1)} %constant_dynamic-slice_fusion), channel_id=1, source_target_pairs={{0,6},{1,7},{2,4},{3,5},{4,2},{5,3},{6,0},{7,1},{8,14},{9,15},{10,... | collective-permute-start | bytes 1572872 | tf_op jit(solution)/shard_map/ppermute | solution.py:253
  11.3 8.3 %collective-permute-start.2 = (bf16[2,128,128]{2,1,0:T(8,128)(2,1)}, bf16[2,128,128]{2,1,0:T(8,128)(2,1)S(1)}, u32[]{:S(2)}, u32[]{:S(2)}) collective-permute-start(bf16[2,128,128]{2,1,0:T(8,128)(2,1)} %get-tuple-element.14), channel_id=1, source_target_pairs={{0,24},{1,25},{2,26},{3,27},{4,28},{5,29},{6,30},{7,31}} | collective-permute-start | bytes 196616 | tf_op jit(solution)/shard_map/ppermute | solution.py:388
  12.5 9.1 %collective-permute-start.1 = (bf16[2,128,128]{2,1,0:T(8,128)(2,1)}, bf16[2,128,128]{2,1,0:T(8,128)(2,1)S(1)}, u32[]{:S(2)}, u32[]{:S(2)}) collective-permute-start(bf16[2,128,128]{2,1,0:T(8,128)(2,1)} %get-tuple-element.14), channel_id=1, source_target_pairs={{0,16},{8,24},{1,17},{9,25},{2,18},{10,26},{3,19},{11,27},{4,20},{... | collective-permute-start | bytes 196616 | tf_op jit(solution)/shard_map/ppermute | solution.py:388
  19.5 6.4 %copy-start.2 = (bf16[2,128,128]{2,1,0:T(8,128)(2,1)}, bf16[2,128,128]{2,1,0:T(8,128)(2,1)S(1)}, u32[]{:S(2)}) copy-start(bf16[2,128,128]{2,1,0:T(8,128)(2,1)S(1)} %collective-permute-done.2.rest_2_) | copy-start | bytes 196612
  19.5 6.4 %collective-permute-start = (bf16[2,128,128]{2,1,0:T(8,128)(2,1)}, bf16[2,128,128]{2,1,0:T(8,128)(2,1)S(1)}, u32[]{:S(2)}, u32[]{:S(2)}) collective-permute-start(bf16[2,128,128]{2,1,0:T(8,128)(2,1)} %get-tuple-element.14), channel_id=1, source_target_pairs={{0,8},{8,16},{16,24},{1,9},{9,17},{17,25},{2,10},{10,18},{18,26},{... | collective-permute-start | bytes 196616 | tf_op jit(solution)/shard_map/ppermute | solution.py:388
  21.6 4.3 %copy-start.3 = (bf16[2,128,128]{2,1,0:T(8,128)(2,1)}, bf16[2,128,128]{2,1,0:T(8,128)(2,1)S(1)}, u32[]{:S(2)}) copy-start(bf16[2,128,128]{2,1,0:T(8,128)(2,1)S(1)} %collective-permute-done.1.rest_1_) | copy-start | bytes 196612
  21.7 56.2 %collective-permute-start.8 = (bf16[256,2048]{1,0:T(8,128)(2,1)}, bf16[256,2048]{1,0:T(8,128)(2,1)}, u32[]{:S(2)}, u32[]{:S(2)}) collective-permute-start(bf16[256,2048]{1,0:T(8,128)(2,1)} %refs_1_.3), channel_id=1, source_target_pairs={{0,1},{1,0},{2,3},{3,2},{4,5},{5,4},{6,7},{7,6},{8,9},{9,8},{10,11... | collective-permute-start | bytes 3145736 | tf_op jit(solution)/shard_map/ppermute | solution.py:253
  25.9 0.6 copy-start.4
  41.6 31.0 %all-to-all-start.1 = ((bf16[8,512,256]{2,1,0:T(8,128)(2,1)}), bf16[8,512,256]{2,1,0:T(8,128)(2,1)}, u32[]{:S(2)}, u32[]{:S(2)}) async-start(bf16[8,512,256]{2,1,0:T(8,128)(2,1)} %get-tuple-element.22), calls=%async_computation.1 | async-start | bytes 4194304 | tf_op jit(solution)/shard_map/all_to_all | solution.py:412
  45.9 22.4 %collective-permute-start.7 = (bf16[128,2048]{1,0:T(8,128)(2,1)}, bf16[128,2048]{1,0:T(8,128)(2,1)}, u32[]{:S(2)}, u32[]{:S(2)}) collective-permute-start(bf16[128,2048]{1,0:T(8,128)(2,1)} %collective-permute-done.4.rest_4_.refs_7_), channel_id=1, source_target_pairs={{0,8},{8,0},{16,24},{24,16},{1,9},{9,1},{17,25},{25,17},{2,10},{10... | collective-permute-start | bytes 1572872 | tf_op jit(solution)/shard_map/ppermute | solution.py:253
  46.0 25.7 %collective-permute-start.6 = (bf16[128,2048]{1,0:T(8,128)(2,1)}, bf16[128,2048]{1,0:T(8,128)(2,1)}, u32[]{:S(2)}, u32[]{:S(2)}) collective-permute-start(bf16[128,2048]{1,0:T(8,128)(2,1)} %collective-permute-done.3.rest_3_.refs_3_), channel_id=1, source_target_pairs={{0,8},{8,0},{16,24},{24,16},{1,9},{9,1},{17,25},{25,17},{2,10},{10... | collective-permute-start | bytes 1572872 | tf_op jit(solution)/shard_map/ppermute | solution.py:253
  48.0 0.8 copy-start
  68.4 8.7 %copy-start.1 = (bf16[128,2048]{1,0:T(8,128)(2,1)S(1)}, bf16[128,2048]{1,0:T(8,128)(2,1)}, u32[]{:S(2)}) copy-start(bf16[128,2048]{1,0:T(8,128)(2,1)} %copy-done) | copy-start | bytes 1572868
  72.6 31.0 %all-to-all-start = ((bf16[8,512,256]{2,1,0:T(8,128)(2,1)}), bf16[8,512,256]{2,1,0:T(8,128)(2,1)}, u32[]{:S(2)}, u32[]{:S(2)}) async-start(bf16[8,512,256]{2,1,0:T(8,128)(2,1)} %get-tuple-element.16), calls=%async_computation | async-start | bytes 4194304 | tf_op jit(solution)/shard_map/all_to_all | solution.py:412
  77.1 2.0 %collective-permute-start.14 = (bf16[128,2048]{1,0:T(8,128)(2,1)S(1)}, bf16[128,2048]{1,0:T(8,128)(2,1)S(1)}, u32[]{:S(2)}, u32[]{:S(2)}) collective-permute-start(bf16[128,2048]{1,0:T(8,128)(2,1)S(1)} %copy-done.1), channel_id=1, source_target_pairs={{0,1},{1,0},{2,3},{3,2},{4,5},{5,4},{6,7},{7,6},{8,9},{9,8},{10,11... | collective-permute-start | bytes 1572872 | tf_op jit(solution)/shard_map/ppermute | solution.py:253
  77.3 14.2 %collective-permute-start.13 = (bf16[128,2048]{1,0:T(8,128)(2,1)S(1)}, bf16[128,2048]{1,0:T(8,128)(2,1)S(1)}, u32[]{:S(2)}, u32[]{:S(2)}) collective-permute-start(bf16[128,2048]{1,0:T(8,128)(2,1)S(1)} %copy-done.1), channel_id=1, source_target_pairs={{0,8},{8,0},{16,24},{24,16},{1,9},{9,1},{17,25},{25,17},{2,10},{10... | collective-permute-start | bytes 1572872 | tf_op jit(solution)/shard_map/ppermute | solution.py:253
  77.3 14.3 %collective-permute-start.9 = (bf16[128,2048]{1,0:T(8,128)(2,1)}, bf16[128,2048]{1,0:T(8,128)(2,1)S(1)}, u32[]{:S(2)}, u32[]{:S(2)}) collective-permute-start(bf16[128,2048]{1,0:T(8,128)(2,1)} %collective-permute-done.3.rest_3_.refs_3_), channel_id=1, source_target_pairs={{0,1},{1,0},{2,3},{3,2},{4,5},{5,4},{6,7},{7,6},{8,9},{9,8},{10,11... | collective-permute-start | bytes 1572872 | tf_op jit(solution)/shard_map/ppermute | solution.py:253
  77.7 13.9 %collective-permute-start.10 = (bf16[128,2048]{1,0:T(8,128)(2,1)}, bf16[128,2048]{1,0:T(8,128)(2,1)S(1)}, u32[]{:S(2)}, u32[]{:S(2)}) collective-permute-start(bf16[128,2048]{1,0:T(8,128)(2,1)} %collective-permute-done.6.refs_4_), channel_id=1, source_target_pairs={{0,1},{1,0},{2,3},{3,2},{4,5},{5,4},{6,7},{7,6},{8,9},{9,8},{10,11... | collective-permute-start | bytes 1572872 | tf_op jit(solution)/shard_map/ppermute | solution.py:253
  77.8 13.8 %collective-permute-start.11 = (bf16[128,2048]{1,0:T(8,128)(2,1)}, bf16[128,2048]{1,0:T(8,128)(2,1)S(1)}, u32[]{:S(2)}, u32[]{:S(2)}) collective-permute-start(bf16[128,2048]{1,0:T(8,128)(2,1)} %collective-permute-done.4.rest_4_.refs_7_), channel_id=1, source_target_pairs={{0,1},{1,0},{2,3},{3,2},{4,5},{5,4},{6,7},{7,6},{8,9},{9,8},{10,11... | collective-permute-start | bytes 1572872 | tf_op jit(solution)/shard_map/ppermute | solution.py:253
  79.1 12.5 %collective-permute-start.12 = (bf16[128,2048]{1,0:T(8,128)(2,1)}, bf16[128,2048]{1,0:T(8,128)(2,1)}, u32[]{:S(2)}, u32[]{:S(2)}) collective-permute-start(bf16[128,2048]{1,0:T(8,128)(2,1)} %collective-permute-done.7.refs_8_), channel_id=1, source_target_pairs={{0,1},{1,0},{2,3},{3,2},{4,5},{5,4},{6,7},{7,6},{8,9},{9,8},{10,11... | collective-permute-start | bytes 1572872 | tf_op jit(solution)/shard_map/ppermute | solution.py:253
  91.5 2.0 %collective-permute-start.15 = (bf16[128,2048]{1,0:T(8,128)(2,1)S(1)}, bf16[128,2048]{1,0:T(8,128)(2,1)}, u32[]{:S(2)}, u32[]{:S(2)}) collective-permute-start(bf16[128,2048]{1,0:T(8,128)(2,1)S(1)} %collective-permute-done.13.refs_12_), channel_id=1, source_target_pairs={{0,1},{1,0},{2,3},{3,2},{4,5},{5,4},{6,7},{7,6},{8,9},{9,8},{10,11... | collective-permute-start | bytes 1572872 | tf_op jit(solution)/shard_map/ppermute | solution.py:253

commit v2 on v1

--- a/solution.py
+++ b/solution.py
@@ -9,11 +9,11 @@
 
 HD = 128
 SEG = 2048
-BLOCK = 256
+BLOCK = 512
 EPS = 1e-06
 LOG2E = 1.4426950408889634
 VMEM = 60 << 20
-PROJECT_VMEM = 44 << 20
+PROJECT_VMEM = 30 << 20
 F32, BF16 = jnp.float32, jnp.bfloat16
 
 
@@ -107,9 +107,12 @@
     return diagonal
 
 
-def local_branch(scores, v, scale_gain):
+def weights_of(scores):
     largest = jnp.max(scores, axis=-1, keepdims=True)
-    weights = jnp.exp2(scores - largest).astype(BF16)
+    return jnp.exp2(scores - largest).astype(BF16)
+
+
+def local_branch(weights, v, scale_gain):
     summed = jnp.dot(
         weights, jnp.concatenate([v, jnp.ones_like(v)], axis=1), preferred_element_type=F32
     )
@@ -124,12 +127,16 @@
         dest, rows, end, head = unit
         return scores_of(q_ref[0, dest, rows, columns(head)], k_ref[:end, columns(head)])
 
-    ahead = make(units[0])
+    ahead, behind = make(units[0]), None
     for unit, following in zip(units, [*units[1:], None]):
         scores = ahead
         if following is not None:
             ahead = make(following)
-        use(unit, scores)
+        weights = weights_of(scores)
+        if behind is not None:
+            use(*behind)
+        behind = unit, weights
+    use(*behind)
 
 
 def memory_branch(q, memory_pair, scale_gain):
@@ -194,11 +201,11 @@
         init_ref, rest[:earlier], term_ref, memory, prefix_ref, prefix_scale
     )
 
-    def use(unit, scores):
+    def use(unit, weights):
         dest, rows, end, head = unit
         cols = columns(head)
         gate = gate_of(beta_ref, head)
-        local = local_branch(scores, v_ref[:end, cols], (1.0 - gate) * loc_gain_ref[:, cols])
+        local = local_branch(weights, v_ref[:end, cols], (1.0 - gate) * loc_gain_ref[:, cols])
         read = memory_branch(q_ref[0, dest, rows, cols], pairs[head], gate * mem_gain_ref[:, cols])
         out_ref[dest, rows, cols] = (read + local).astype(BF16)
 
@@ -213,7 +220,8 @@
     start, size = block
     q = query.reshape(segs, dests, per_dest, width)
     q_block = tuple(map(pl.Element, (1, dests, size, width)))
-    segment = pl.BlockSpec((SEG, width), lambda seg: (seg, 0))
+    met = (dests - 1) * per_dest + start + size
+    segment = pl.BlockSpec((pl.Element(met), pl.Element(width)), lambda seg: (seg * SEG, 0))
     prefix_shape = (1, heads, HD, HD)
     pairs_met = segs * heads * size * sum(dest * per_dest + start + size for dest in range(dests))
     return call(
@@ -297,12 +305,20 @@
         for part in range(parts):
             at, row = len(copies), turn * width + part * size
             copies.append(pltpu.make_async_copy(w_refs[at], w_held.at[row : row + size], sems.at[at]))
-            copies[-1].start()
             place = part if parts == 1 else place_ref[1] ^ part
             places.append((turn, source, pl.ds(pl.multiple_of(place * size, size), size)))
-    row_copy.wait()
     step = len(parts_of) // groups
     strip = out_width // groups
+
+    def fetch(group):
+        for copy, (turn, _, _) in zip(copies, places):
+            if turn // step == group:
+                copy.start()
+
+    ahead = 2
+    for group in range(min(ahead, groups)):
+        fetch(group)
+    row_copy.wait()
     sends = []
     for group in range(groups):
         found = []
@@ -310,6 +326,8 @@
             if turn // step == group:
                 copy.wait()
                 found.append(row_held[source, :, cols])
+        if group + ahead < groups:
+            fetch(group + ahead)
         rows = jnp.concatenate(found, axis=1)
         met = slice(group * step * width, (group + 1) * step * width)
         for at in range(groups):

time: 113 us -> 111 us (0.982)
  no operation moved by 1% of the time
where the time goes in v2:
time: 111 us
  Pallas kernels  57.1 us (51%)
  waiting for transfers between devices  31.2 us (28%)
  starting transfers between devices  19 us (17%)
  local copies, waits for them, and re-layouts  2.55 us (2%)
    pallas_call x2, Pallas kernels, chunk_call(): call(functools.partial(chunk_body, block, per_dest, tokens ** (-0.5), len...  33.9 us
    ppermute x13, waiting for transfers between devices, flip(): return lax.ppermute(array, axis, [(at, at ^ turn) for at in range(size)])  18.8 us
    pallas_call x2, Pallas kernels, project(): pl.pallas_call(functools.partial(project_body, parts_of=tuple(map(len, pi...  17.2 us
    ppermute x3, waiting for transfers between devices, per_device(): lax.ppermute(total, 'seq', [(at, at + step) for at in range(seq_size - st...  10.8 us
    all_to_all x2, starting transfers between devices, per_device(): lax.all_to_all(chunk, 'head', split_axis=0, concat_axis=0, tiled=True)  8.13 us
    ppermute x13, starting transfers between devices, flip(): return lax.ppermute(array, axis, [(at, at ^ turn) for at in range(size)])  7.03 us
    pallas_call x1, Pallas kernels, kv_terms(): call(kv_body, 'kv_terms', (jax.ShapeDtypeStruct((segs, heads, HD, HD), F3...  5.97 us
    ppermute x3, starting transfers between devices, per_device(): lax.ppermute(total, 'seq', [(at, at + step) for at in range(seq_size - st...  3.85 us
  transfers between devices with their start and end apart: 18, of which 9 were waited for; matrix products, arithmetic and copies ran while one was open for 0% of the time, Pallas kernels for 44%

profile of v2, /device:TPU:24, one launch (start us, length us, event | category | flops | bytes accessed | tf_op | source)
XLA Modules:
  0.0 110.9 jit_solution(6220950248860450604)
XLA Ops:
  0.6 1.1 constant_dynamic-slice_fusion
  1.7 1.6 %collective-permute-start.4 = (bf16[128,2048]{1,0:T(8,128)(2,1)S(1)}, bf16[128,2048]{1,0:T(8,128)(2,1)}, u32[]{:S(2)}, u32[]{:S(2)}) collective-permute-start(bf16[128,2048]{1,0:T(8,128)(2,1)S(1)} %constant_dynamic-slice_fusion), channel_id=1, source_target_pairs={{0,4},{1,5},{2,6},{3,7},{4,0},{5,1},{6,2},{7,3},{8,12},{9,13},{10,... | collective-permute-start | bytes 1572872 | tf_op jit(solution)/shard_map/ppermute | solution.py:261
  3.3 1.5 %collective-permute-start.3 = (bf16[128,2048]{1,0:T(8,128)(2,1)S(1)}, bf16[128,2048]{1,0:T(8,128)(2,1)}, u32[]{:S(2)}, u32[]{:S(2)}) collective-permute-start(bf16[128,2048]{1,0:T(8,128)(2,1)S(1)} %constant_dynamic-slice_fusion), channel_id=1, source_target_pairs={{0,2},{1,3},{2,0},{3,1},{4,6},{5,7},{6,4},{7,5},{8,10},{9,11},{10,... | collective-permute-start | bytes 1572872 | tf_op jit(solution)/shard_map/ppermute | solution.py:261
  4.8 0.5 collective-permute-start.5
  5.3 6.0 %kv_terms.1 = (f32[4,2,128,128]{3,2,1,0:T(8,128)}, bf16[2,128,128]{2,1,0:T(8,128)(2,1)}) custom-call(bf16[8192,256]{1,0:T(8,128)(2,1)} %k_ref.5, bf16[8192,256]{1,0:T(8,128)(2,1)} %v_ref.5), custom_call_target="tpu_custom_call" | custom-call | flops 536870912 | bytes 8388608 | tf_op jit(solution)/shard_map/kv_terms/pallas_call | solution.py:66
  11.3 1.3 %collective-permute-start.2 = (bf16[2,128,128]{2,1,0:T(8,128)(2,1)}, bf16[2,128,128]{2,1,0:T(8,128)(2,1)S(1)}, u32[]{:S(2)}, u32[]{:S(2)}) collective-permute-start(bf16[2,128,128]{2,1,0:T(8,128)(2,1)} %get-tuple-element.14), channel_id=1, source_target_pairs={{0,24},{1,25},{2,26},{3,27},{4,28},{5,29},{6,30},{7,31}} | collective-permute-start | bytes 196616 | tf_op jit(solution)/shard_map/ppermute | solution.py:406
  12.5 1.3 %collective-permute-start.1 = (bf16[2,128,128]{2,1,0:T(8,128)(2,1)}, bf16[2,128,128]{2,1,0:T(8,128)(2,1)S(1)}, u32[]{:S(2)}, u32[]{:S(2)}) collective-permute-start(bf16[2,128,128]{2,1,0:T(8,128)(2,1)} %get-tuple-element.14), channel_id=1, source_target_pairs={{0,16},{8,24},{1,17},{9,25},{2,18},{10,26},{3,19},{11,27},{4,20},{... | collective-permute-start | bytes 196616 | tf_op jit(solution)/shard_map/ppermute | solution.py:406
  13.8 5.7 %collective-permute-done.2.rest_2_ = bf16[2,128,128]{2,1,0:T(8,128)(2,1)S(1)} collective-permute-done((bf16[2,128,128]{2,1,0:T(8,128)(2,1)}, bf16[2,128,128]{2,1,0:T(8,128)(2,1)S(1)}, u32[]{:S(2)}, u32[]{:S(2)}) %collective-permute-start.2) | collective-permute-done | bytes 65568 | tf_op jit(solution)/shard_map/ppermute | solution.py:406
  19.5 1.3 %collective-permute-start = (bf16[2,128,128]{2,1,0:T(8,128)(2,1)}, bf16[2,128,128]{2,1,0:T(8,128)(2,1)S(1)}, u32[]{:S(2)}, u32[]{:S(2)}) collective-permute-start(bf16[2,128,128]{2,1,0:T(8,128)(2,1)} %get-tuple-element.14), channel_id=1, source_target_pairs={{0,8},{8,16},{16,24},{1,9},{9,17},{17,25},{2,10},{10,18},{18,26},{... | collective-permute-start | bytes 196616 | tf_op jit(solution)/shard_map/ppermute | solution.py:406
  20.8 0.8 collective-permute-done.1.rest_1_
  21.7 4.3 %collective-permute-done.rest_0_ = bf16[2,128,128]{2,1,0:T(8,128)(2,1)S(1)} collective-permute-done((bf16[2,128,128]{2,1,0:T(8,128)(2,1)}, bf16[2,128,128]{2,1,0:T(8,128)(2,1)S(1)}, u32[]{:S(2)}, u32[]{:S(2)}) %collective-permute-start) | collective-permute-done | bytes 65568 | tf_op jit(solution)/shard_map/ppermute | solution.py:406
  25.9 0.6 copy-done.4
  26.5 14.6 %attention.3 = (bf16[8,512,256]{2,1,0:T(8,128)(2,1)}, f32[1,2,128,128]{3,2,1,0:T(8,128)}) custom-call(bf16[4,2,1024,256]{3,2,1,0:T(8,128)(2,1)} %bitcast.5, bf16[8192,256]{1,0:T(8,128)(2,1)} %k_ref.5, bf16[8192,256]{1,0:T(8,128)(2,1)} %v_ref.5, f32[2,128,128]{2,1,0:T(8,128)} %init_ref.3, f32[4,2,128,128]{3,2,1,0:T(8,128)} %get-tuple-element.13.term_ref, ...), custom_call_target="tpu_custom_call" | custom-call | flops 85899344 | bytes 125829 | tf_op jit(solution)/shard_map/attention/pallas_call | solution.py:227
  41.2 4.3 %all-to-all-start.1 = ((bf16[8,512,256]{2,1,0:T(8,128)(2,1)}), bf16[8,512,256]{2,1,0:T(8,128)(2,1)}, u32[]{:S(2)}, u32[]{:S(2)}) async-start(bf16[8,512,256]{2,1,0:T(8,128)(2,1)} %get-tuple-element.22), calls=%async_computation.1 | async-start | bytes 4194304 | tf_op jit(solution)/shard_map/all_to_all | solution.py:430
  45.6 2.0 %collective-permute-start.6 = (bf16[128,2048]{1,0:T(8,128)(2,1)}, bf16[128,2048]{1,0:T(8,128)(2,1)}, u32[]{:S(2)}, u32[]{:S(2)}) collective-permute-start(bf16[128,2048]{1,0:T(8,128)(2,1)} %collective-permute-done.3.rest_3_.refs_3_), channel_id=1, source_target_pairs={{0,8},{8,0},{16,24},{24,16},{1,9},{9,1},{17,25},{25,17},{2,10},{10... | collective-permute-start | bytes 1572872 | tf_op jit(solution)/shard_map/ppermute | solution.py:261
  47.7 0.8 copy-done
  48.5 19.3 %attention.2 = (bf16[8,512,256]{2,1,0:T(8,128)(2,1)}, f32[1,2,128,128]{3,2,1,0:T(8,128)}) custom-call(bf16[4,2,1024,256]{3,2,1,0:T(8,128)(2,1)} %bitcast.6, bf16[8192,256]{1,0:T(8,128)(2,1)} %k_ref.5, bf16[8192,256]{1,0:T(8,128)(2,1)} %v_ref.5, f32[2,128,128]{2,1,0:T(8,128)} %init_ref.3, f32[4,2,128,128]{3,2,1,0:T(8,128)} %get-tuple-element.13.term_ref, ...), custom_call_target="tpu_custom_call" | custom-call | flops 257698037760 | bytes 251658240 | tf_op jit(solution)/shard_map/attention/pallas_call | solution.py:227
  67.8 3.5 %collective-permute-done.6.refs_4_ = bf16[128,2048]{1,0:T(8,128)(2,1)} collective-permute-done((bf16[128,2048]{1,0:T(8,128)(2,1)}, bf16[128,2048]{1,0:T(8,128)(2,1)}, u32[]{:S(2)}, u32[]{:S(2)}) %collective-permute-start.6) | collective-permute-done | bytes 524320 | tf_op jit(solution)/shard_map/ppermute | solution.py:261
  71.3 0.9 all-to-all-done.1.refs_0_
  72.2 3.8 %all-to-all-start = ((bf16[8,512,256]{2,1,0:T(8,128)(2,1)}), bf16[8,512,256]{2,1,0:T(8,128)(2,1)S(1)}, u32[]{:S(2)}, u32[]{:S(2)}) async-start(bf16[8,512,256]{2,1,0:T(8,128)(2,1)} %get-tuple-element.16), calls=%async_computation | async-start | bytes 4194304 | tf_op jit(solution)/shard_map/all_to_all | solution.py:430
  76.0 0.2 collective-permute-start.14
  76.2 0.4 collective-permute-start.9
  76.6 0.2 collective-permute-start.10
  76.7 0.4 collective-permute-start.11
  77.1 0.9 collective-permute-done.14.refs_13_
  78.0 0.3 collective-permute-start.12
  78.2 12.2 %collective-permute-done.13.refs_12_ = bf16[128,2048]{1,0:T(8,128)(2,1)} collective-permute-done((bf16[128,2048]{1,0:T(8,128)(2,1)S(1)}, bf16[128,2048]{1,0:T(8,128)(2,1)}, u32[]{:S(2)}, u32[]{:S(2)}) %collective-permute-start.13) | collective-permute-done | bytes 524320 | tf_op jit(solution)/shard_map/ppermute | solution.py:261
  90.5 0.1 pad_add_fusion.place_ref
  90.6 2.2 %collective-permute-done.15.refs_14_ = bf16[128,2048]{1,0:T(8,128)(2,1)} collective-permute-done((bf16[128,2048]{1,0:T(8,128)(2,1)}, bf16[128,2048]{1,0:T(8,128)(2,1)}, u32[]{:S(2)}, u32[]{:S(2)}) %collective-permute-start.15) | collective-permute-done | bytes 524320 | tf_op jit(solution)/shard_map/ppermute | solution.py:261
  92.7 8.8 %project.2.refs_15_ = bf16[1024,2048]{1,0:T(8,128)(2,1)} custom-call(s32[2]{0:T(128)S(1)} %pad_add_fusion.place_ref, bf16[8,512,256]{2,1,0:T(8,128)(2,1)} %all-to-all-done.1.refs_0_, bf16[256,2048]{1,0:T(8,128)(2,1)} %refs_1_.3, bf16[256,2048]{1,0:T(8,128)(2,1)} %collective-permute-done.8.refs_2_, bf16[128,2048]{1,0:T(8,128)(2,1)} %collective-permute-done.3.rest_3_.refs_3_, ...), custom_call_target="tpu_custom_call" | custom-call | flops 4294967296 | bytes 12582912 | tf_op jit(solution)/shard_map/project/pallas_call | solution.py:362
  101.6 0.8 all-to-all-done.refs_0_
  102.4 8.3 %project.3 = bf16[1024,2048]{1,0:T(8,128)(2,1)} custom-call(s32[2]{0:T(128)S(1)} %pad_add_fusion.place_ref, bf16[8,512,256]{2,1,0:T(8,128)(2,1)S(1)} %all-to-all-done.refs_0_, bf16[256,2048]{1,0:T(8,128)(2,1)} %refs_1_.3, bf16[256,2048]{1,0:T(8,128)(2,1)} %collective-permute-done.8.refs_2_, ...), custom_call_target="tpu_custom_call", output_to_operand_aliasing={{}: (16, {})} | custom-call | flops 4294967296 | bytes 12582912 | tf_op jit(solution)/shard_map/project/pallas_call | solution.py:362
  (21 shorter events, 0.1 us)
Async XLA Ops:
  1.7 43.8 %collective-permute-start.4 = (bf16[128,2048]{1,0:T(8,128)(2,1)S(1)}, bf16[128,2048]{1,0:T(8,128)(2,1)}, u32[]{:S(2)}, u32[]{:S(2)}) collective-permute-start(bf16[128,2048]{1,0:T(8,128)(2,1)S(1)} %constant_dynamic-slice_fusion), channel_id=1, source_target_pairs={{0,4},{1,5},{2,6},{3,7},{4,0},{5,1},{6,2},{7,3},{8,12},{9,13},{10,... | collective-permute-start | bytes 1572872 | tf_op jit(solution)/shard_map/ppermute | solution.py:261
  3.3 42.3 %collective-permute-start.3 = (bf16[128,2048]{1,0:T(8,128)(2,1)S(1)}, bf16[128,2048]{1,0:T(8,128)(2,1)}, u32[]{:S(2)}, u32[]{:S(2)}) collective-permute-start(bf16[128,2048]{1,0:T(8,128)(2,1)S(1)} %constant_dynamic-slice_fusion), channel_id=1, source_target_pairs={{0,2},{1,3},{2,0},{3,1},{4,6},{5,7},{6,4},{7,5},{8,10},{9,11},{10,... | collective-permute-start | bytes 1572872 | tf_op jit(solution)/shard_map/ppermute | solution.py:261
  4.8 42.8 %collective-permute-start.5 = (bf16[128,2048]{1,0:T(8,128)(2,1)S(1)}, bf16[128,2048]{1,0:T(8,128)(2,1)S(1)}, u32[]{:S(2)}, u32[]{:S(2)}) collective-permute-start(bf16[128,2048]{1,0:T(8,128)(2,1)S(1)} %constant_dynamic-slice_fusion), channel_id=1, source_target_pairs={{0,6},{1,7},{2,4},{3,5},{4,2},{5,3},{6,0},{7,1},{8,14},{9,15},{10,... | collective-permute-start | bytes 1572872 | tf_op jit(solution)/shard_map/ppermute | solution.py:261
  11.3 8.3 %collective-permute-start.2 = (bf16[2,128,128]{2,1,0:T(8,128)(2,1)}, bf16[2,128,128]{2,1,0:T(8,128)(2,1)S(1)}, u32[]{:S(2)}, u32[]{:S(2)}) collective-permute-start(bf16[2,128,128]{2,1,0:T(8,128)(2,1)} %get-tuple-element.14), channel_id=1, source_target_pairs={{0,24},{1,25},{2,26},{3,27},{4,28},{5,29},{6,30},{7,31}} | collective-permute-start | bytes 196616 | tf_op jit(solution)/shard_map/ppermute | solution.py:406
  12.5 9.1 %collective-permute-start.1 = (bf16[2,128,128]{2,1,0:T(8,128)(2,1)}, bf16[2,128,128]{2,1,0:T(8,128)(2,1)S(1)}, u32[]{:S(2)}, u32[]{:S(2)}) collective-permute-start(bf16[2,128,128]{2,1,0:T(8,128)(2,1)} %get-tuple-element.14), channel_id=1, source_target_pairs={{0,16},{8,24},{1,17},{9,25},{2,18},{10,26},{3,19},{11,27},{4,20},{... | collective-permute-start | bytes 196616 | tf_op jit(solution)/shard_map/ppermute | solution.py:406
  19.5 6.4 %copy-start.2 = (bf16[2,128,128]{2,1,0:T(8,128)(2,1)}, bf16[2,128,128]{2,1,0:T(8,128)(2,1)S(1)}, u32[]{:S(2)}) copy-start(bf16[2,128,128]{2,1,0:T(8,128)(2,1)S(1)} %collective-permute-done.2.rest_2_) | copy-start | bytes 196612
  19.5 6.4 %collective-permute-start = (bf16[2,128,128]{2,1,0:T(8,128)(2,1)}, bf16[2,128,128]{2,1,0:T(8,128)(2,1)S(1)}, u32[]{:S(2)}, u32[]{:S(2)}) collective-permute-start(bf16[2,128,128]{2,1,0:T(8,128)(2,1)} %get-tuple-element.14), channel_id=1, source_target_pairs={{0,8},{8,16},{16,24},{1,9},{9,17},{17,25},{2,10},{10,18},{18,26},{... | collective-permute-start | bytes 196616 | tf_op jit(solution)/shard_map/ppermute | solution.py:406
  21.6 4.3 %copy-start.3 = (bf16[2,128,128]{2,1,0:T(8,128)(2,1)}, bf16[2,128,128]{2,1,0:T(8,128)(2,1)S(1)}, u32[]{:S(2)}) copy-start(bf16[2,128,128]{2,1,0:T(8,128)(2,1)S(1)} %collective-permute-done.1.rest_1_) | copy-start | bytes 196612
  21.7 55.1 %collective-permute-start.8 = (bf16[256,2048]{1,0:T(8,128)(2,1)}, bf16[256,2048]{1,0:T(8,128)(2,1)}, u32[]{:S(2)}, u32[]{:S(2)}) collective-permute-start(bf16[256,2048]{1,0:T(8,128)(2,1)} %refs_1_.3), channel_id=1, source_target_pairs={{0,1},{1,0},{2,3},{3,2},{4,5},{5,4},{6,7},{7,6},{8,9},{9,8},{10,11... | collective-permute-start | bytes 3145736 | tf_op jit(solution)/shard_map/ppermute | solution.py:261
  25.9 0.6 copy-start.4
  41.2 31.0 %all-to-all-start.1 = ((bf16[8,512,256]{2,1,0:T(8,128)(2,1)}), bf16[8,512,256]{2,1,0:T(8,128)(2,1)}, u32[]{:S(2)}, u32[]{:S(2)}) async-start(bf16[8,512,256]{2,1,0:T(8,128)(2,1)} %get-tuple-element.22), calls=%async_computation.1 | async-start | bytes 4194304 | tf_op jit(solution)/shard_map/all_to_all | solution.py:430
  45.5 22.3 %collective-permute-start.7 = (bf16[128,2048]{1,0:T(8,128)(2,1)}, bf16[128,2048]{1,0:T(8,128)(2,1)}, u32[]{:S(2)}, u32[]{:S(2)}) collective-permute-start(bf16[128,2048]{1,0:T(8,128)(2,1)} %collective-permute-done.4.rest_4_.refs_7_), channel_id=1, source_target_pairs={{0,8},{8,0},{16,24},{24,16},{1,9},{9,1},{17,25},{25,17},{2,10},{10... | collective-permute-start | bytes 1572872 | tf_op jit(solution)/shard_map/ppermute | solution.py:261
  45.6 25.7 %collective-permute-start.6 = (bf16[128,2048]{1,0:T(8,128)(2,1)}, bf16[128,2048]{1,0:T(8,128)(2,1)}, u32[]{:S(2)}, u32[]{:S(2)}) collective-permute-start(bf16[128,2048]{1,0:T(8,128)(2,1)} %collective-permute-done.3.rest_3_.refs_3_), channel_id=1, source_target_pairs={{0,8},{8,0},{16,24},{24,16},{1,9},{9,1},{17,25},{25,17},{2,10},{10... | collective-permute-start | bytes 1572872 | tf_op jit(solution)/shard_map/ppermute | solution.py:261
  47.7 0.9 copy-start
  67.8 8.2 %copy-start.1 = (bf16[128,2048]{1,0:T(8,128)(2,1)S(1)}, bf16[128,2048]{1,0:T(8,128)(2,1)}, u32[]{:S(2)}) copy-start(bf16[128,2048]{1,0:T(8,128)(2,1)} %copy-done) | copy-start | bytes 1572868
  72.2 30.2 %all-to-all-start = ((bf16[8,512,256]{2,1,0:T(8,128)(2,1)}), bf16[8,512,256]{2,1,0:T(8,128)(2,1)S(1)}, u32[]{:S(2)}, u32[]{:S(2)}) async-start(bf16[8,512,256]{2,1,0:T(8,128)(2,1)} %get-tuple-element.16), calls=%async_computation | async-start | bytes 4194304 | tf_op jit(solution)/shard_map/all_to_all | solution.py:430
  76.0 2.0 %collective-permute-start.14 = (bf16[128,2048]{1,0:T(8,128)(2,1)S(1)}, bf16[128,2048]{1,0:T(8,128)(2,1)S(1)}, u32[]{:S(2)}, u32[]{:S(2)}) collective-permute-start(bf16[128,2048]{1,0:T(8,128)(2,1)S(1)} %copy-done.1), channel_id=1, source_target_pairs={{0,1},{1,0},{2,3},{3,2},{4,5},{5,4},{6,7},{7,6},{8,9},{9,8},{10,11... | collective-permute-start | bytes 1572872 | tf_op jit(solution)/shard_map/ppermute | solution.py:261
  76.2 14.3 %collective-permute-start.13 = (bf16[128,2048]{1,0:T(8,128)(2,1)S(1)}, bf16[128,2048]{1,0:T(8,128)(2,1)}, u32[]{:S(2)}, u32[]{:S(2)}) collective-permute-start(bf16[128,2048]{1,0:T(8,128)(2,1)S(1)} %copy-done.1), channel_id=1, source_target_pairs={{0,8},{8,0},{16,24},{24,16},{1,9},{9,1},{17,25},{25,17},{2,10},{10... | collective-permute-start | bytes 1572872 | tf_op jit(solution)/shard_map/ppermute | solution.py:261
  76.2 14.4 %collective-permute-start.9 = (bf16[128,2048]{1,0:T(8,128)(2,1)}, bf16[128,2048]{1,0:T(8,128)(2,1)}, u32[]{:S(2)}, u32[]{:S(2)}) collective-permute-start(bf16[128,2048]{1,0:T(8,128)(2,1)} %collective-permute-done.3.rest_3_.refs_3_), channel_id=1, source_target_pairs={{0,1},{1,0},{2,3},{3,2},{4,5},{5,4},{6,7},{7,6},{8,9},{9,8},{10,11... | collective-permute-start | bytes 1572872 | tf_op jit(solution)/shard_map/ppermute | solution.py:261
  76.6 14.0 %collective-permute-start.10 = (bf16[128,2048]{1,0:T(8,128)(2,1)}, bf16[128,2048]{1,0:T(8,128)(2,1)}, u32[]{:S(2)}, u32[]{:S(2)}) collective-permute-start(bf16[128,2048]{1,0:T(8,128)(2,1)} %collective-permute-done.6.refs_4_), channel_id=1, source_target_pairs={{0,1},{1,0},{2,3},{3,2},{4,5},{5,4},{6,7},{7,6},{8,9},{9,8},{10,11... | collective-permute-start | bytes 1572872 | tf_op jit(solution)/shard_map/ppermute | solution.py:261
  76.7 13.9 %collective-permute-start.11 = (bf16[128,2048]{1,0:T(8,128)(2,1)}, bf16[128,2048]{1,0:T(8,128)(2,1)}, u32[]{:S(2)}, u32[]{:S(2)}) collective-permute-start(bf16[128,2048]{1,0:T(8,128)(2,1)} %collective-permute-done.4.rest_4_.refs_7_), channel_id=1, source_target_pairs={{0,1},{1,0},{2,3},{3,2},{4,5},{5,4},{6,7},{7,6},{8,9},{9,8},{10,11... | collective-permute-start | bytes 1572872 | tf_op jit(solution)/shard_map/ppermute | solution.py:261
  78.0 12.6 %collective-permute-start.12 = (bf16[128,2048]{1,0:T(8,128)(2,1)}, bf16[128,2048]{1,0:T(8,128)(2,1)}, u32[]{:S(2)}, u32[]{:S(2)}) collective-permute-start(bf16[128,2048]{1,0:T(8,128)(2,1)} %collective-permute-done.7.refs_8_), channel_id=1, source_target_pairs={{0,1},{1,0},{2,3},{3,2},{4,5},{5,4},{6,7},{7,6},{8,9},{9,8},{10,11... | collective-permute-start | bytes 1572872 | tf_op jit(solution)/shard_map/ppermute | solution.py:261
  90.5 2.3 %collective-permute-start.15 = (bf16[128,2048]{1,0:T(8,128)(2,1)}, bf16[128,2048]{1,0:T(8,128)(2,1)}, u32[]{:S(2)}, u32[]{:S(2)}) collective-permute-start(bf16[128,2048]{1,0:T(8,128)(2,1)} %collective-permute-done.13.refs_12_), channel_id=1, source_target_pairs={{0,1},{1,0},{2,3},{3,2},{4,5},{5,4},{6,7},{7,6},{8,9},{9,8},{10,11... | collective-permute-start | bytes 1572872 | tf_op jit(solution)/shard_map/ppermute | solution.py:261

commit v3 on v2

--- a/solution.py
+++ b/solution.py
@@ -12,7 +12,7 @@
 BLOCK = 512
 EPS = 1e-06
 LOG2E = 1.4426950408889634
-VMEM = 60 << 20
+VMEM = 51 << 20
 PROJECT_VMEM = 30 << 20
 F32, BF16 = jnp.float32, jnp.bfloat16
 

time: 111 us -> 109 us (0.982)
  local copies, waits for them, and re-layouts: 2.55 us -> 1.11 us
    unnamed x10 -> x8, local copies, waits for them, and re-layouts: 1.47 us -> 0.03 us
where the time goes in v3:
time: 109 us
  Pallas kernels  56.1 us (51%)
  waiting for transfers between devices  31.8 us (29%)
  starting transfers between devices  19 us (17%)
  local copies, waits for them, and re-layouts  1.11 us (1%)
    pallas_call x2, Pallas kernels, chunk_call(): call(functools.partial(chunk_body, block, per_dest, tokens ** (-0.5), len...  33.7 us
    ppermute x13, waiting for transfers between devices, flip(): return lax.ppermute(array, axis, [(at, at ^ turn) for at in range(size)])  19.8 us
    pallas_call x2, Pallas kernels, project(): pl.pallas_call(functools.partial(project_body, parts_of=tuple(map(len, pi...  17.2 us
    ppermute x3, waiting for transfers between devices, per_device(): lax.ppermute(total, 'seq', [(at, at + step) for at in range(seq_size - st...  10.3 us
    all_to_all x2, starting transfers between devices, per_device(): lax.all_to_all(chunk, 'head', split_axis=0, concat_axis=0, tiled=True)  8.13 us
    ppermute x13, starting transfers between devices, flip(): return lax.ppermute(array, axis, [(at, at ^ turn) for at in range(size)])  7.03 us
    pallas_call x1, Pallas kernels, kv_terms(): call(kv_body, 'kv_terms', (jax.ShapeDtypeStruct((segs, heads, HD, HD), F3...  5.25 us
    ppermute x3, starting transfers between devices, per_device(): lax.ppermute(total, 'seq', [(at, at + step) for at in range(seq_size - st...  3.86 us
  transfers between devices with their start and end apart: 18, of which 9 were waited for; matrix products, arithmetic and copies ran while one was open for 0% of the time, Pallas kernels for 44%

profile of v3, /device:TPU:24, one launch (start us, length us, event | category | flops | bytes accessed | tf_op | source)
XLA Modules:
  0.0 109.1 jit_solution(11903085595695291540)
XLA Ops:
  0.6 1.1 constant_dynamic-slice_fusion
  1.8 0.0 copy-start.1
  1.8 1.6 %collective-permute-start.4 = (bf16[128,2048]{1,0:T(8,128)(2,1)S(1)}, bf16[128,2048]{1,0:T(8,128)(2,1)}, u32[]{:S(2)}, u32[]{:S(2)}) collective-permute-start(bf16[128,2048]{1,0:T(8,128)(2,1)S(1)} %constant_dynamic-slice_fusion), channel_id=1, source_target_pairs={{0,4},{1,5},{2,6},{3,7},{4,0},{5,1},{6,2},{7,3},{8,12},{9,13},{10,... | collective-permute-start | bytes 1572872 | tf_op jit(solution)/shard_map/ppermute | solution.py:261
  3.4 1.5 %collective-permute-start.3 = (bf16[128,2048]{1,0:T(8,128)(2,1)S(1)}, bf16[128,2048]{1,0:T(8,128)(2,1)}, u32[]{:S(2)}, u32[]{:S(2)}) collective-permute-start(bf16[128,2048]{1,0:T(8,128)(2,1)S(1)} %constant_dynamic-slice_fusion), channel_id=1, source_target_pairs={{0,2},{1,3},{2,0},{3,1},{4,6},{5,7},{6,4},{7,5},{8,10},{9,11},{10,... | collective-permute-start | bytes 1572872 | tf_op jit(solution)/shard_map/ppermute | solution.py:261
  4.9 0.5 collective-permute-start.5
  5.3 5.3 %kv_terms.1 = (f32[4,2,128,128]{3,2,1,0:T(8,128)S(1)}, bf16[2,128,128]{2,1,0:T(8,128)(2,1)S(1)}) custom-call(bf16[8192,256]{1,0:T(8,128)(2,1)} %k_ref.5, bf16[8192,256]{1,0:T(8,128)(2,1)} %v_ref.5), custom_call_target="tpu_custom_call" | custom-call | flops 536870912 | bytes 8388608 | tf_op jit(solution)/shard_map/kv_terms/pallas_call | solution.py:66
  10.6 1.3 %collective-permute-start.2 = (bf16[2,128,128]{2,1,0:T(8,128)(2,1)S(1)}, bf16[2,128,128]{2,1,0:T(8,128)(2,1)S(1)}, u32[]{:S(2)}, u32[]{:S(2)}) collective-permute-start(bf16[2,128,128]{2,1,0:T(8,128)(2,1)S(1)} %get-tuple-element.14), channel_id=1, source_target_pairs={{0,24},{1,25},{2,26},{3,27},{4,28},{5,29},{6,30},{7,31}} | collective-permute-start | bytes 196616 | tf_op jit(solution)/shard_map/ppermute | solution.py:406
  11.9 1.3 %collective-permute-start.1 = (bf16[2,128,128]{2,1,0:T(8,128)(2,1)S(1)}, bf16[2,128,128]{2,1,0:T(8,128)(2,1)S(1)}, u32[]{:S(2)}, u32[]{:S(2)}) collective-permute-start(bf16[2,128,128]{2,1,0:T(8,128)(2,1)S(1)} %get-tuple-element.14), channel_id=1, source_target_pairs={{0,16},{8,24},{1,17},{9,25},{2,18},{10,26},{3,19},{11,27},{4,20},{... | collective-permute-start | bytes 196616 | tf_op jit(solution)/shard_map/ppermute | solution.py:406
  13.2 5.5 %collective-permute-done.2.rest_2_ = bf16[2,128,128]{2,1,0:T(8,128)(2,1)S(1)} collective-permute-done((bf16[2,128,128]{2,1,0:T(8,128)(2,1)S(1)}, bf16[2,128,128]{2,1,0:T(8,128)(2,1)S(1)}, u32[]{:S(2)}, u32[]{:S(2)}) %collective-permute-start.2) | collective-permute-done | bytes 65568 | tf_op jit(solution)/shard_map/ppermute | solution.py:406
  18.7 1.3 %collective-permute-start = (bf16[2,128,128]{2,1,0:T(8,128)(2,1)S(1)}, bf16[2,128,128]{2,1,0:T(8,128)(2,1)S(1)}, u32[]{:S(2)}, u32[]{:S(2)}) collective-permute-start(bf16[2,128,128]{2,1,0:T(8,128)(2,1)S(1)} %get-tuple-element.14), channel_id=1, source_target_pairs={{0,8},{8,16},{16,24},{1,9},{9,17},{17,25},{2,10},{10,18},{18,26},{... | collective-permute-start | bytes 196616 | tf_op jit(solution)/shard_map/ppermute | solution.py:406
  20.0 0.8 collective-permute-done.1.rest_1_
  20.8 4.0 %collective-permute-done.rest_0_ = bf16[2,128,128]{2,1,0:T(8,128)(2,1)S(1)} collective-permute-done((bf16[2,128,128]{2,1,0:T(8,128)(2,1)S(1)}, bf16[2,128,128]{2,1,0:T(8,128)(2,1)S(1)}, u32[]{:S(2)}, u32[]{:S(2)}) %collective-permute-start) | collective-permute-done | bytes 65568 | tf_op jit(solution)/shard_map/ppermute | solution.py:406
  24.9 14.5 %attention.3 = (bf16[8,512,256]{2,1,0:T(8,128)(2,1)}, f32[1,2,128,128]{3,2,1,0:T(8,128)}) custom-call(bf16[4,2,1024,256]{3,2,1,0:T(8,128)(2,1)} %bitcast.9, bf16[8192,256]{1,0:T(8,128)(2,1)} %k_ref.5, bf16[8192,256]{1,0:T(8,128)(2,1)} %v_ref.5, f32[2,128,128]{2,1,0:T(8,128)S(1)} %copy-done, f32[4,2,128,128]{3,2,1,0:T(8,128)S(1)} %get-tuple-element.13.term_ref, ...), custom_call_target="tpu_custom_call" | custom-call | flops 85899344 | bytes 125829 | tf_op jit(solution)/shard_map/attention/pallas_call | solution.py:227
  39.4 4.4 %all-to-all-start.1 = ((bf16[8,512,256]{2,1,0:T(8,128)(2,1)}), bf16[8,512,256]{2,1,0:T(8,128)(2,1)}, u32[]{:S(2)}, u32[]{:S(2)}) async-start(bf16[8,512,256]{2,1,0:T(8,128)(2,1)} %get-tuple-element.22), calls=%async_computation.1 | async-start | bytes 4194304 | tf_op jit(solution)/shard_map/all_to_all | solution.py:430
  43.7 0.1 collective-permute-start.7
  43.8 2.0 %collective-permute-start.6 = (bf16[128,2048]{1,0:T(8,128)(2,1)}, bf16[128,2048]{1,0:T(8,128)(2,1)}, u32[]{:S(2)}, u32[]{:S(2)}) collective-permute-start(bf16[128,2048]{1,0:T(8,128)(2,1)} %collective-permute-done.3.rest_3_.refs_3_), channel_id=1, source_target_pairs={{0,8},{8,0},{16,24},{24,16},{1,9},{9,1},{17,25},{25,17},{2,10},{10... | collective-permute-start | bytes 1572872 | tf_op jit(solution)/shard_map/ppermute | solution.py:261
  45.9 19.1 %attention.2 = (bf16[8,512,256]{2,1,0:T(8,128)(2,1)}, f32[1,2,128,128]{3,2,1,0:T(8,128)}) custom-call(bf16[4,2,1024,256]{3,2,1,0:T(8,128)(2,1)} %bitcast.10, bf16[8192,256]{1,0:T(8,128)(2,1)} %k_ref.5, bf16[8192,256]{1,0:T(8,128)(2,1)} %v_ref.5, f32[2,128,128]{2,1,0:T(8,128)S(1)} %copy-done, f32[4,2,128,128]{3,2,1,0:T(8,128)S(1)} %get-tuple-element.13.term_ref, ...), custom_call_target="tpu_custom_call" | custom-call | flops 257698037760 | bytes 251658240 | tf_op jit(solution)/shard_map/attention/pallas_call | solution.py:227
  65.0 4.5 %collective-permute-done.6.refs_4_ = bf16[128,2048]{1,0:T(8,128)(2,1)} collective-permute-done((bf16[128,2048]{1,0:T(8,128)(2,1)}, bf16[128,2048]{1,0:T(8,128)(2,1)}, u32[]{:S(2)}, u32[]{:S(2)}) %collective-permute-start.6) | collective-permute-done | bytes 524320 | tf_op jit(solution)/shard_map/ppermute | solution.py:261
  69.5 0.9 all-to-all-done.1.refs_0_
  70.4 3.8 %all-to-all-start = ((bf16[8,512,256]{2,1,0:T(8,128)(2,1)}), bf16[8,512,256]{2,1,0:T(8,128)(2,1)S(1)}, u32[]{:S(2)}, u32[]{:S(2)}) async-start(bf16[8,512,256]{2,1,0:T(8,128)(2,1)} %get-tuple-element.16), calls=%async_computation | async-start | bytes 4194304 | tf_op jit(solution)/shard_map/all_to_all | solution.py:430
  74.2 0.2 collective-permute-start.14
  74.4 0.4 collective-permute-start.9
  74.8 0.2 collective-permute-start.10
  74.9 0.4 collective-permute-start.11
  75.3 0.9 collective-permute-done.14.refs_13_
  76.2 0.3 collective-permute-start.12
  76.5 12.2 %collective-permute-done.13.refs_12_ = bf16[128,2048]{1,0:T(8,128)(2,1)} collective-permute-done((bf16[128,2048]{1,0:T(8,128)(2,1)S(1)}, bf16[128,2048]{1,0:T(8,128)(2,1)}, u32[]{:S(2)}, u32[]{:S(2)}) %collective-permute-start.13) | collective-permute-done | bytes 524320 | tf_op jit(solution)/shard_map/ppermute | solution.py:261
  88.7 0.1 pad_add_fusion.place_ref
  88.8 2.2 %collective-permute-done.15.refs_14_ = bf16[128,2048]{1,0:T(8,128)(2,1)} collective-permute-done((bf16[128,2048]{1,0:T(8,128)(2,1)}, bf16[128,2048]{1,0:T(8,128)(2,1)}, u32[]{:S(2)}, u32[]{:S(2)}) %collective-permute-start.15) | collective-permute-done | bytes 524320 | tf_op jit(solution)/shard_map/ppermute | solution.py:261
  90.9 8.8 %project.2.refs_15_ = bf16[1024,2048]{1,0:T(8,128)(2,1)} custom-call(s32[2]{0:T(128)S(1)} %pad_add_fusion.place_ref, bf16[8,512,256]{2,1,0:T(8,128)(2,1)} %all-to-all-done.1.refs_0_, bf16[256,2048]{1,0:T(8,128)(2,1)} %refs_1_.3, bf16[256,2048]{1,0:T(8,128)(2,1)} %collective-permute-done.8.refs_2_, bf16[128,2048]{1,0:T(8,128)(2,1)} %collective-permute-done.3.rest_3_.refs_3_, ...), custom_call_target="tpu_custom_call" | custom-call | flops 4294967296 | bytes 12582912 | tf_op jit(solution)/shard_map/project/pallas_call | solution.py:362
  99.8 0.8 all-to-all-done.refs_0_
  100.6 8.3 %project.3 = bf16[1024,2048]{1,0:T(8,128)(2,1)} custom-call(s32[2]{0:T(128)S(1)} %pad_add_fusion.place_ref, bf16[8,512,256]{2,1,0:T(8,128)(2,1)S(1)} %all-to-all-done.refs_0_, bf16[256,2048]{1,0:T(8,128)(2,1)} %refs_1_.3, bf16[256,2048]{1,0:T(8,128)(2,1)} %collective-permute-done.8.refs_2_, ...), custom_call_target="tpu_custom_call", output_to_operand_aliasing={{}: (16, {})} | custom-call | flops 4294967296 | bytes 12582912 | tf_op jit(solution)/shard_map/project/pallas_call | solution.py:362
  (19 shorter events, 0.1 us)
Async XLA Ops:
  1.7 23.1 %copy-start = (f32[2,128,128]{2,1,0:T(8,128)S(1)}, f32[2,128,128]{2,1,0:T(8,128)}, u32[]{:S(2)}) copy-start(f32[2,128,128]{2,1,0:T(8,128)} %init_ref.3) | copy-start | bytes 393220
  1.8 23.1 %copy-start.1 = (f32[256]{0:T(256)S(1)}, f32[256]{0:T(256)}, u32[]{:S(2)}) copy-start(f32[256]{0:T(256)} %param.13) | copy-start | bytes 3076
  1.8 23.1 %copy-start.2 = (f32[256]{0:T(256)S(1)}, f32[256]{0:T(256)}, u32[]{:S(2)}) copy-start(f32[256]{0:T(256)} %param.14) | copy-start | bytes 3076
  1.8 23.1 %copy-start.3 = (f32[2]{0:T(128)S(1)}, f32[2]{0:T(128)}, u32[]{:S(2)}) copy-start(f32[2]{0:T(128)} %beta_ref.3) | copy-start | bytes 28
  1.8 42.0 %collective-permute-start.4 = (bf16[128,2048]{1,0:T(8,128)(2,1)S(1)}, bf16[128,2048]{1,0:T(8,128)(2,1)}, u32[]{:S(2)}, u32[]{:S(2)}) collective-permute-start(bf16[128,2048]{1,0:T(8,128)(2,1)S(1)} %constant_dynamic-slice_fusion), channel_id=1, source_target_pairs={{0,4},{1,5},{2,6},{3,7},{4,0},{5,1},{6,2},{7,3},{8,12},{9,13},{10,... | collective-permute-start | bytes 1572872 | tf_op jit(solution)/shard_map/ppermute | solution.py:261
  3.4 40.5 %collective-permute-start.3 = (bf16[128,2048]{1,0:T(8,128)(2,1)S(1)}, bf16[128,2048]{1,0:T(8,128)(2,1)}, u32[]{:S(2)}, u32[]{:S(2)}) collective-permute-start(bf16[128,2048]{1,0:T(8,128)(2,1)S(1)} %constant_dynamic-slice_fusion), channel_id=1, source_target_pairs={{0,2},{1,3},{2,0},{3,1},{4,6},{5,7},{6,4},{7,5},{8,10},{9,11},{10,... | collective-permute-start | bytes 1572872 | tf_op jit(solution)/shard_map/ppermute | solution.py:261
  4.9 41.0 %collective-permute-start.5 = (bf16[128,2048]{1,0:T(8,128)(2,1)S(1)}, bf16[128,2048]{1,0:T(8,128)(2,1)S(1)}, u32[]{:S(2)}, u32[]{:S(2)}) collective-permute-start(bf16[128,2048]{1,0:T(8,128)(2,1)S(1)} %constant_dynamic-slice_fusion), channel_id=1, source_target_pairs={{0,6},{1,7},{2,4},{3,5},{4,2},{5,3},{6,0},{7,1},{8,14},{9,15},{10,... | collective-permute-start | bytes 1572872 | tf_op jit(solution)/shard_map/ppermute | solution.py:261
  10.6 8.1 %collective-permute-start.2 = (bf16[2,128,128]{2,1,0:T(8,128)(2,1)S(1)}, bf16[2,128,128]{2,1,0:T(8,128)(2,1)S(1)}, u32[]{:S(2)}, u32[]{:S(2)}) collective-permute-start(bf16[2,128,128]{2,1,0:T(8,128)(2,1)S(1)} %get-tuple-element.14), channel_id=1, source_target_pairs={{0,24},{1,25},{2,26},{3,27},{4,28},{5,29},{6,30},{7,31}} | collective-permute-start | bytes 196616 | tf_op jit(solution)/shard_map/ppermute | solution.py:406
  11.9 8.9 %collective-permute-start.1 = (bf16[2,128,128]{2,1,0:T(8,128)(2,1)S(1)}, bf16[2,128,128]{2,1,0:T(8,128)(2,1)S(1)}, u32[]{:S(2)}, u32[]{:S(2)}) collective-permute-start(bf16[2,128,128]{2,1,0:T(8,128)(2,1)S(1)} %get-tuple-element.14), channel_id=1, source_target_pairs={{0,16},{8,24},{1,17},{9,25},{2,18},{10,26},{3,19},{11,27},{4,20},{... | collective-permute-start | bytes 196616 | tf_op jit(solution)/shard_map/ppermute | solution.py:406
  18.7 6.1 %collective-permute-start = (bf16[2,128,128]{2,1,0:T(8,128)(2,1)S(1)}, bf16[2,128,128]{2,1,0:T(8,128)(2,1)S(1)}, u32[]{:S(2)}, u32[]{:S(2)}) collective-permute-start(bf16[2,128,128]{2,1,0:T(8,128)(2,1)S(1)} %get-tuple-element.14), channel_id=1, source_target_pairs={{0,8},{8,16},{16,24},{1,9},{9,17},{17,25},{2,10},{10,18},{18,26},{... | collective-permute-start | bytes 196616 | tf_op jit(solution)/shard_map/ppermute | solution.py:406
  20.8 54.1 %collective-permute-start.8 = (bf16[256,2048]{1,0:T(8,128)(2,1)}, bf16[256,2048]{1,0:T(8,128)(2,1)}, u32[]{:S(2)}, u32[]{:S(2)}) collective-permute-start(bf16[256,2048]{1,0:T(8,128)(2,1)} %refs_1_.3), channel_id=1, source_target_pairs={{0,1},{1,0},{2,3},{3,2},{4,5},{5,4},{6,7},{7,6},{8,9},{9,8},{10,11... | collective-permute-start | bytes 3145736 | tf_op jit(solution)/shard_map/ppermute | solution.py:261
  39.4 31.0 %all-to-all-start.1 = ((bf16[8,512,256]{2,1,0:T(8,128)(2,1)}), bf16[8,512,256]{2,1,0:T(8,128)(2,1)}, u32[]{:S(2)}, u32[]{:S(2)}) async-start(bf16[8,512,256]{2,1,0:T(8,128)(2,1)} %get-tuple-element.22), calls=%async_computation.1 | async-start | bytes 4194304 | tf_op jit(solution)/shard_map/all_to_all | solution.py:430
  43.7 21.3 %collective-permute-start.7 = (bf16[128,2048]{1,0:T(8,128)(2,1)}, bf16[128,2048]{1,0:T(8,128)(2,1)}, u32[]{:S(2)}, u32[]{:S(2)}) collective-permute-start(bf16[128,2048]{1,0:T(8,128)(2,1)} %collective-permute-done.4.rest_4_.refs_7_), channel_id=1, source_target_pairs={{0,8},{8,0},{16,24},{24,16},{1,9},{9,1},{17,25},{25,17},{2,10},{10... | collective-permute-start | bytes 1572872 | tf_op jit(solution)/shard_map/ppermute | solution.py:261
  43.8 25.7 %collective-permute-start.6 = (bf16[128,2048]{1,0:T(8,128)(2,1)}, bf16[128,2048]{1,0:T(8,128)(2,1)}, u32[]{:S(2)}, u32[]{:S(2)}) collective-permute-start(bf16[128,2048]{1,0:T(8,128)(2,1)} %collective-permute-done.3.rest_3_.refs_3_), channel_id=1, source_target_pairs={{0,8},{8,0},{16,24},{24,16},{1,9},{9,1},{17,25},{25,17},{2,10},{10... | collective-permute-start | bytes 1572872 | tf_op jit(solution)/shard_map/ppermute | solution.py:261
  70.4 30.2 %all-to-all-start = ((bf16[8,512,256]{2,1,0:T(8,128)(2,1)}), bf16[8,512,256]{2,1,0:T(8,128)(2,1)S(1)}, u32[]{:S(2)}, u32[]{:S(2)}) async-start(bf16[8,512,256]{2,1,0:T(8,128)(2,1)} %get-tuple-element.16), calls=%async_computation | async-start | bytes 4194304 | tf_op jit(solution)/shard_map/all_to_all | solution.py:430
  74.2 2.0 %collective-permute-start.14 = (bf16[128,2048]{1,0:T(8,128)(2,1)S(1)}, bf16[128,2048]{1,0:T(8,128)(2,1)S(1)}, u32[]{:S(2)}, u32[]{:S(2)}) collective-permute-start(bf16[128,2048]{1,0:T(8,128)(2,1)S(1)} %collective-permute-done.5.rest_5_.refs_11_), channel_id=1, source_target_pairs={{0,1},{1,0},{2,3},{3,2},{4,5},{5,4},{6,7},{7,6},{8,9},{9,8},{10,11... | collective-permute-start | bytes 1572872 | tf_op jit(solution)/shard_map/ppermute | solution.py:261
  74.4 14.3 %collective-permute-start.13 = (bf16[128,2048]{1,0:T(8,128)(2,1)S(1)}, bf16[128,2048]{1,0:T(8,128)(2,1)}, u32[]{:S(2)}, u32[]{:S(2)}) collective-permute-start(bf16[128,2048]{1,0:T(8,128)(2,1)S(1)} %collective-permute-done.5.rest_5_.refs_11_), channel_id=1, source_target_pairs={{0,8},{8,0},{16,24},{24,16},{1,9},{9,1},{17,25},{25,17},{2,10},{10... | collective-permute-start | bytes 1572872 | tf_op jit(solution)/shard_map/ppermute | solution.py:261
  74.4 14.4 %collective-permute-start.9 = (bf16[128,2048]{1,0:T(8,128)(2,1)}, bf16[128,2048]{1,0:T(8,128)(2,1)}, u32[]{:S(2)}, u32[]{:S(2)}) collective-permute-start(bf16[128,2048]{1,0:T(8,128)(2,1)} %collective-permute-done.3.rest_3_.refs_3_), channel_id=1, source_target_pairs={{0,1},{1,0},{2,3},{3,2},{4,5},{5,4},{6,7},{7,6},{8,9},{9,8},{10,11... | collective-permute-start | bytes 1572872 | tf_op jit(solution)/shard_map/ppermute | solution.py:261
  74.8 14.0 %collective-permute-start.10 = (bf16[128,2048]{1,0:T(8,128)(2,1)}, bf16[128,2048]{1,0:T(8,128)(2,1)}, u32[]{:S(2)}, u32[]{:S(2)}) collective-permute-start(bf16[128,2048]{1,0:T(8,128)(2,1)} %collective-permute-done.6.refs_4_), channel_id=1, source_target_pairs={{0,1},{1,0},{2,3},{3,2},{4,5},{5,4},{6,7},{7,6},{8,9},{9,8},{10,11... | collective-permute-start | bytes 1572872 | tf_op jit(solution)/shard_map/ppermute | solution.py:261
  74.9 13.9 %collective-permute-start.11 = (bf16[128,2048]{1,0:T(8,128)(2,1)}, bf16[128,2048]{1,0:T(8,128)(2,1)}, u32[]{:S(2)}, u32[]{:S(2)}) collective-permute-start(bf16[128,2048]{1,0:T(8,128)(2,1)} %collective-permute-done.4.rest_4_.refs_7_), channel_id=1, source_target_pairs={{0,1},{1,0},{2,3},{3,2},{4,5},{5,4},{6,7},{7,6},{8,9},{9,8},{10,11... | collective-permute-start | bytes 1572872 | tf_op jit(solution)/shard_map/ppermute | solution.py:261
  76.2 12.6 %collective-permute-start.12 = (bf16[128,2048]{1,0:T(8,128)(2,1)}, bf16[128,2048]{1,0:T(8,128)(2,1)}, u32[]{:S(2)}, u32[]{:S(2)}) collective-permute-start(bf16[128,2048]{1,0:T(8,128)(2,1)} %collective-permute-done.7.refs_8_), channel_id=1, source_target_pairs={{0,1},{1,0},{2,3},{3,2},{4,5},{5,4},{6,7},{7,6},{8,9},{9,8},{10,11... | collective-permute-start | bytes 1572872 | tf_op jit(solution)/shard_map/ppermute | solution.py:261
  88.7 2.3 %collective-permute-start.15 = (bf16[128,2048]{1,0:T(8,128)(2,1)}, bf16[128,2048]{1,0:T(8,128)(2,1)}, u32[]{:S(2)}, u32[]{:S(2)}) collective-permute-start(bf16[128,2048]{1,0:T(8,128)(2,1)} %collective-permute-done.13.refs_12_), channel_id=1, source_target_pairs={{0,1},{1,0},{2,3},{3,2},{4,5},{5,4},{6,7},{7,6},{8,9},{9,8},{10,11... | collective-permute-start | bytes 1572872 | tf_op jit(solution)/shard_map/ppermute | solution.py:261

commit v4 on v3

--- a/solution.py
+++ b/solution.py
@@ -315,7 +315,7 @@
             if turn // step == group:
                 copy.start()
 
-    ahead = 2
+    ahead = 3
     for group in range(min(ahead, groups)):
         fetch(group)
     row_copy.wait()

time: 109 us -> 109 us (level)
  no operation moved by 1% of the time
where the time goes in v4:
time: 109 us
  Pallas kernels  56.1 us (51%)
  waiting for transfers between devices  31.8 us (29%)
  starting transfers between devices  19 us (17%)
  local copies, waits for them, and re-layouts  1.11 us (1%)
    pallas_call x2, Pallas kernels, chunk_call(): call(functools.partial(chunk_body, block, per_dest, tokens ** (-0.5), len...  33.7 us
    ppermute x13, waiting for transfers between devices, flip(): return lax.ppermute(array, axis, [(at, at ^ turn) for at in range(size)])  19.8 us
    pallas_call x2, Pallas kernels, project(): pl.pallas_call(functools.partial(project_body, parts_of=tuple(map(len, pi...  17.2 us
    ppermute x3, waiting for transfers between devices, per_device(): lax.ppermute(total, 'seq', [(at, at + step) for at in range(seq_size - st...  10.3 us
    all_to_all x2, starting transfers between devices, per_device(): lax.all_to_all(chunk, 'head', split_axis=0, concat_axis=0, tiled=True)  8.13 us
    ppermute x13, starting transfers between devices, flip(): return lax.ppermute(array, axis, [(at, at ^ turn) for at in range(size)])  7.03 us
    pallas_call x1, Pallas kernels, kv_terms(): call(kv_body, 'kv_terms', (jax.ShapeDtypeStruct((segs, heads, HD, HD), F3...  5.25 us
    ppermute x3, starting transfers between devices, per_device(): lax.ppermute(total, 'seq', [(at, at + step) for at in range(seq_size - st...  3.86 us
  transfers between devices with their start and end apart: 18, of which 9 were waited for; matrix products, arithmetic and copies ran while one was open for 0% of the time, Pallas kernels for 44%

profile of v4, /device:TPU:24, one launch (start us, length us, event | category | flops | bytes accessed | tf_op | source)
XLA Modules:
  0.0 109.1 jit_solution(9676083966649769444)
XLA Ops:
  0.6 1.1 constant_dynamic-slice_fusion
  1.7 0.0 copy-start
  1.8 1.6 %collective-permute-start.4 = (bf16[128,2048]{1,0:T(8,128)(2,1)S(1)}, bf16[128,2048]{1,0:T(8,128)(2,1)}, u32[]{:S(2)}, u32[]{:S(2)}) collective-permute-start(bf16[128,2048]{1,0:T(8,128)(2,1)S(1)} %constant_dynamic-slice_fusion), channel_id=1, source_target_pairs={{0,4},{1,5},{2,6},{3,7},{4,0},{5,1},{6,2},{7,3},{8,12},{9,13},{10,... | collective-permute-start | bytes 1572872 | tf_op jit(solution)/shard_map/ppermute | solution.py:261
  3.4 1.5 %collective-permute-start.3 = (bf16[128,2048]{1,0:T(8,128)(2,1)S(1)}, bf16[128,2048]{1,0:T(8,128)(2,1)}, u32[]{:S(2)}, u32[]{:S(2)}) collective-permute-start(bf16[128,2048]{1,0:T(8,128)(2,1)S(1)} %constant_dynamic-slice_fusion), channel_id=1, source_target_pairs={{0,2},{1,3},{2,0},{3,1},{4,6},{5,7},{6,4},{7,5},{8,10},{9,11},{10,... | collective-permute-start | bytes 1572872 | tf_op jit(solution)/shard_map/ppermute | solution.py:261
  4.9 0.5 collective-permute-start.5
  5.3 5.3 %kv_terms.1 = (f32[4,2,128,128]{3,2,1,0:T(8,128)S(1)}, bf16[2,128,128]{2,1,0:T(8,128)(2,1)S(1)}) custom-call(bf16[8192,256]{1,0:T(8,128)(2,1)} %k_ref.5, bf16[8192,256]{1,0:T(8,128)(2,1)} %v_ref.5), custom_call_target="tpu_custom_call" | custom-call | flops 536870912 | bytes 8388608 | tf_op jit(solution)/shard_map/kv_terms/pallas_call | solution.py:66
  10.6 1.3 %collective-permute-start.2 = (bf16[2,128,128]{2,1,0:T(8,128)(2,1)S(1)}, bf16[2,128,128]{2,1,0:T(8,128)(2,1)S(1)}, u32[]{:S(2)}, u32[]{:S(2)}) collective-permute-start(bf16[2,128,128]{2,1,0:T(8,128)(2,1)S(1)} %get-tuple-element.14), channel_id=1, source_target_pairs={{0,24},{1,25},{2,26},{3,27},{4,28},{5,29},{6,30},{7,31}} | collective-permute-start | bytes 196616 | tf_op jit(solution)/shard_map/ppermute | solution.py:406
  11.9 1.3 %collective-permute-start.1 = (bf16[2,128,128]{2,1,0:T(8,128)(2,1)S(1)}, bf16[2,128,128]{2,1,0:T(8,128)(2,1)S(1)}, u32[]{:S(2)}, u32[]{:S(2)}) collective-permute-start(bf16[2,128,128]{2,1,0:T(8,128)(2,1)S(1)} %get-tuple-element.14), channel_id=1, source_target_pairs={{0,16},{8,24},{1,17},{9,25},{2,18},{10,26},{3,19},{11,27},{4,20},{... | collective-permute-start | bytes 196616 | tf_op jit(solution)/shard_map/ppermute | solution.py:406
  13.2 5.5 %collective-permute-done.2.rest_2_ = bf16[2,128,128]{2,1,0:T(8,128)(2,1)S(1)} collective-permute-done((bf16[2,128,128]{2,1,0:T(8,128)(2,1)S(1)}, bf16[2,128,128]{2,1,0:T(8,128)(2,1)S(1)}, u32[]{:S(2)}, u32[]{:S(2)}) %collective-permute-start.2) | collective-permute-done | bytes 65568 | tf_op jit(solution)/shard_map/ppermute | solution.py:406
  18.7 1.3 %collective-permute-start = (bf16[2,128,128]{2,1,0:T(8,128)(2,1)S(1)}, bf16[2,128,128]{2,1,0:T(8,128)(2,1)S(1)}, u32[]{:S(2)}, u32[]{:S(2)}) collective-permute-start(bf16[2,128,128]{2,1,0:T(8,128)(2,1)S(1)} %get-tuple-element.14), channel_id=1, source_target_pairs={{0,8},{8,16},{16,24},{1,9},{9,17},{17,25},{2,10},{10,18},{18,26},{... | collective-permute-start | bytes 196616 | tf_op jit(solution)/shard_map/ppermute | solution.py:406
  20.0 0.8 collective-permute-done.1.rest_1_
  20.8 4.0 %collective-permute-done.rest_0_ = bf16[2,128,128]{2,1,0:T(8,128)(2,1)S(1)} collective-permute-done((bf16[2,128,128]{2,1,0:T(8,128)(2,1)S(1)}, bf16[2,128,128]{2,1,0:T(8,128)(2,1)S(1)}, u32[]{:S(2)}, u32[]{:S(2)}) %collective-permute-start) | collective-permute-done | bytes 65568 | tf_op jit(solution)/shard_map/ppermute | solution.py:406
  24.9 14.5 %attention.3 = (bf16[8,512,256]{2,1,0:T(8,128)(2,1)}, f32[1,2,128,128]{3,2,1,0:T(8,128)}) custom-call(bf16[4,2,1024,256]{3,2,1,0:T(8,128)(2,1)} %bitcast.9, bf16[8192,256]{1,0:T(8,128)(2,1)} %k_ref.5, bf16[8192,256]{1,0:T(8,128)(2,1)} %v_ref.5, f32[2,128,128]{2,1,0:T(8,128)S(1)} %copy-done, f32[4,2,128,128]{3,2,1,0:T(8,128)S(1)} %get-tuple-element.13.term_ref, ...), custom_call_target="tpu_custom_call" | custom-call | flops 85899344 | bytes 125829 | tf_op jit(solution)/shard_map/attention/pallas_call | solution.py:227
  39.4 4.4 %all-to-all-start.1 = ((bf16[8,512,256]{2,1,0:T(8,128)(2,1)}), bf16[8,512,256]{2,1,0:T(8,128)(2,1)}, u32[]{:S(2)}, u32[]{:S(2)}) async-start(bf16[8,512,256]{2,1,0:T(8,128)(2,1)} %get-tuple-element.22), calls=%async_computation.1 | async-start | bytes 4194304 | tf_op jit(solution)/shard_map/all_to_all | solution.py:430
  43.7 0.1 collective-permute-start.7
  43.8 2.0 %collective-permute-start.6 = (bf16[128,2048]{1,0:T(8,128)(2,1)}, bf16[128,2048]{1,0:T(8,128)(2,1)}, u32[]{:S(2)}, u32[]{:S(2)}) collective-permute-start(bf16[128,2048]{1,0:T(8,128)(2,1)} %collective-permute-done.3.rest_3_.refs_3_), channel_id=1, source_target_pairs={{0,8},{8,0},{16,24},{24,16},{1,9},{9,1},{17,25},{25,17},{2,10},{10... | collective-permute-start | bytes 1572872 | tf_op jit(solution)/shard_map/ppermute | solution.py:261
  45.9 19.1 %attention.2 = (bf16[8,512,256]{2,1,0:T(8,128)(2,1)}, f32[1,2,128,128]{3,2,1,0:T(8,128)}) custom-call(bf16[4,2,1024,256]{3,2,1,0:T(8,128)(2,1)} %bitcast.10, bf16[8192,256]{1,0:T(8,128)(2,1)} %k_ref.5, bf16[8192,256]{1,0:T(8,128)(2,1)} %v_ref.5, f32[2,128,128]{2,1,0:T(8,128)S(1)} %copy-done, f32[4,2,128,128]{3,2,1,0:T(8,128)S(1)} %get-tuple-element.13.term_ref, ...), custom_call_target="tpu_custom_call" | custom-call | flops 257698037760 | bytes 251658240 | tf_op jit(solution)/shard_map/attention/pallas_call | solution.py:227
  65.0 4.5 %collective-permute-done.6.refs_4_ = bf16[128,2048]{1,0:T(8,128)(2,1)} collective-permute-done((bf16[128,2048]{1,0:T(8,128)(2,1)}, bf16[128,2048]{1,0:T(8,128)(2,1)}, u32[]{:S(2)}, u32[]{:S(2)}) %collective-permute-start.6) | collective-permute-done | bytes 524320 | tf_op jit(solution)/shard_map/ppermute | solution.py:261
  69.5 0.9 all-to-all-done.1.refs_0_
  70.4 3.8 %all-to-all-start = ((bf16[8,512,256]{2,1,0:T(8,128)(2,1)}), bf16[8,512,256]{2,1,0:T(8,128)(2,1)S(1)}, u32[]{:S(2)}, u32[]{:S(2)}) async-start(bf16[8,512,256]{2,1,0:T(8,128)(2,1)} %get-tuple-element.16), calls=%async_computation | async-start | bytes 4194304 | tf_op jit(solution)/shard_map/all_to_all | solution.py:430
  74.2 0.2 collective-permute-start.14
  74.4 0.4 collective-permute-start.9
  74.8 0.2 collective-permute-start.10
  74.9 0.4 collective-permute-start.11
  75.3 0.9 collective-permute-done.14.refs_13_
  76.2 0.3 collective-permute-start.12
  76.5 12.2 %collective-permute-done.13.refs_12_ = bf16[128,2048]{1,0:T(8,128)(2,1)} collective-permute-done((bf16[128,2048]{1,0:T(8,128)(2,1)S(1)}, bf16[128,2048]{1,0:T(8,128)(2,1)}, u32[]{:S(2)}, u32[]{:S(2)}) %collective-permute-start.13) | collective-permute-done | bytes 524320 | tf_op jit(solution)/shard_map/ppermute | solution.py:261
  88.7 0.1 pad_add_fusion.place_ref
  88.8 2.2 %collective-permute-done.15.refs_14_ = bf16[128,2048]{1,0:T(8,128)(2,1)} collective-permute-done((bf16[128,2048]{1,0:T(8,128)(2,1)}, bf16[128,2048]{1,0:T(8,128)(2,1)}, u32[]{:S(2)}, u32[]{:S(2)}) %collective-permute-start.15) | collective-permute-done | bytes 524320 | tf_op jit(solution)/shard_map/ppermute | solution.py:261
  90.9 8.8 %project.2.refs_15_ = bf16[1024,2048]{1,0:T(8,128)(2,1)} custom-call(s32[2]{0:T(128)S(1)} %pad_add_fusion.place_ref, bf16[8,512,256]{2,1,0:T(8,128)(2,1)} %all-to-all-done.1.refs_0_, bf16[256,2048]{1,0:T(8,128)(2,1)} %refs_1_.3, bf16[256,2048]{1,0:T(8,128)(2,1)} %collective-permute-done.8.refs_2_, bf16[128,2048]{1,0:T(8,128)(2,1)} %collective-permute-done.3.rest_3_.refs_3_, ...), custom_call_target="tpu_custom_call" | custom-call | flops 4294967296 | bytes 12582912 | tf_op jit(solution)/shard_map/project/pallas_call | solution.py:362
  99.8 0.8 all-to-all-done.refs_0_
  100.6 8.3 %project.3 = bf16[1024,2048]{1,0:T(8,128)(2,1)} custom-call(s32[2]{0:T(128)S(1)} %pad_add_fusion.place_ref, bf16[8,512,256]{2,1,0:T(8,128)(2,1)S(1)} %all-to-all-done.refs_0_, bf16[256,2048]{1,0:T(8,128)(2,1)} %refs_1_.3, bf16[256,2048]{1,0:T(8,128)(2,1)} %collective-permute-done.8.refs_2_, ...), custom_call_target="tpu_custom_call", output_to_operand_aliasing={{}: (16, {})} | custom-call | flops 4294967296 | bytes 12582912 | tf_op jit(solution)/shard_map/project/pallas_call | solution.py:362
  (19 shorter events, 0.1 us)
Async XLA Ops:
  1.7 23.1 %copy-start = (f32[2,128,128]{2,1,0:T(8,128)S(1)}, f32[2,128,128]{2,1,0:T(8,128)}, u32[]{:S(2)}) copy-start(f32[2,128,128]{2,1,0:T(8,128)} %init_ref.3) | copy-start | bytes 393220
  1.8 23.1 %copy-start.1 = (f32[256]{0:T(256)S(1)}, f32[256]{0:T(256)}, u32[]{:S(2)}) copy-start(f32[256]{0:T(256)} %param.13) | copy-start | bytes 3076
  1.8 23.1 %copy-start.2 = (f32[256]{0:T(256)S(1)}, f32[256]{0:T(256)}, u32[]{:S(2)}) copy-start(f32[256]{0:T(256)} %param.14) | copy-start | bytes 3076
  1.8 23.1 %copy-start.3 = (f32[2]{0:T(128)S(1)}, f32[2]{0:T(128)}, u32[]{:S(2)}) copy-start(f32[2]{0:T(128)} %beta_ref.3) | copy-start | bytes 28
  1.8 42.0 %collective-permute-start.4 = (bf16[128,2048]{1,0:T(8,128)(2,1)S(1)}, bf16[128,2048]{1,0:T(8,128)(2,1)}, u32[]{:S(2)}, u32[]{:S(2)}) collective-permute-start(bf16[128,2048]{1,0:T(8,128)(2,1)S(1)} %constant_dynamic-slice_fusion), channel_id=1, source_target_pairs={{0,4},{1,5},{2,6},{3,7},{4,0},{5,1},{6,2},{7,3},{8,12},{9,13},{10,... | collective-permute-start | bytes 1572872 | tf_op jit(solution)/shard_map/ppermute | solution.py:261
  3.4 40.5 %collective-permute-start.3 = (bf16[128,2048]{1,0:T(8,128)(2,1)S(1)}, bf16[128,2048]{1,0:T(8,128)(2,1)}, u32[]{:S(2)}, u32[]{:S(2)}) collective-permute-start(bf16[128,2048]{1,0:T(8,128)(2,1)S(1)} %constant_dynamic-slice_fusion), channel_id=1, source_target_pairs={{0,2},{1,3},{2,0},{3,1},{4,6},{5,7},{6,4},{7,5},{8,10},{9,11},{10,... | collective-permute-start | bytes 1572872 | tf_op jit(solution)/shard_map/ppermute | solution.py:261
  4.9 41.0 %collective-permute-start.5 = (bf16[128,2048]{1,0:T(8,128)(2,1)S(1)}, bf16[128,2048]{1,0:T(8,128)(2,1)S(1)}, u32[]{:S(2)}, u32[]{:S(2)}) collective-permute-start(bf16[128,2048]{1,0:T(8,128)(2,1)S(1)} %constant_dynamic-slice_fusion), channel_id=1, source_target_pairs={{0,6},{1,7},{2,4},{3,5},{4,2},{5,3},{6,0},{7,1},{8,14},{9,15},{10,... | collective-permute-start | bytes 1572872 | tf_op jit(solution)/shard_map/ppermute | solution.py:261
  10.6 8.1 %collective-permute-start.2 = (bf16[2,128,128]{2,1,0:T(8,128)(2,1)S(1)}, bf16[2,128,128]{2,1,0:T(8,128)(2,1)S(1)}, u32[]{:S(2)}, u32[]{:S(2)}) collective-permute-start(bf16[2,128,128]{2,1,0:T(8,128)(2,1)S(1)} %get-tuple-element.14), channel_id=1, source_target_pairs={{0,24},{1,25},{2,26},{3,27},{4,28},{5,29},{6,30},{7,31}} | collective-permute-start | bytes 196616 | tf_op jit(solution)/shard_map/ppermute | solution.py:406
  11.9 8.9 %collective-permute-start.1 = (bf16[2,128,128]{2,1,0:T(8,128)(2,1)S(1)}, bf16[2,128,128]{2,1,0:T(8,128)(2,1)S(1)}, u32[]{:S(2)}, u32[]{:S(2)}) collective-permute-start(bf16[2,128,128]{2,1,0:T(8,128)(2,1)S(1)} %get-tuple-element.14), channel_id=1, source_target_pairs={{0,16},{8,24},{1,17},{9,25},{2,18},{10,26},{3,19},{11,27},{4,20},{... | collective-permute-start | bytes 196616 | tf_op jit(solution)/shard_map/ppermute | solution.py:406
  18.7 6.1 %collective-permute-start = (bf16[2,128,128]{2,1,0:T(8,128)(2,1)S(1)}, bf16[2,128,128]{2,1,0:T(8,128)(2,1)S(1)}, u32[]{:S(2)}, u32[]{:S(2)}) collective-permute-start(bf16[2,128,128]{2,1,0:T(8,128)(2,1)S(1)} %get-tuple-element.14), channel_id=1, source_target_pairs={{0,8},{8,16},{16,24},{1,9},{9,17},{17,25},{2,10},{10,18},{18,26},{... | collective-permute-start | bytes 196616 | tf_op jit(solution)/shard_map/ppermute | solution.py:406
  20.8 54.1 %collective-permute-start.8 = (bf16[256,2048]{1,0:T(8,128)(2,1)}, bf16[256,2048]{1,0:T(8,128)(2,1)}, u32[]{:S(2)}, u32[]{:S(2)}) collective-permute-start(bf16[256,2048]{1,0:T(8,128)(2,1)} %refs_1_.3), channel_id=1, source_target_pairs={{0,1},{1,0},{2,3},{3,2},{4,5},{5,4},{6,7},{7,6},{8,9},{9,8},{10,11... | collective-permute-start | bytes 3145736 | tf_op jit(solution)/shard_map/ppermute | solution.py:261
  39.4 31.0 %all-to-all-start.1 = ((bf16[8,512,256]{2,1,0:T(8,128)(2,1)}), bf16[8,512,256]{2,1,0:T(8,128)(2,1)}, u32[]{:S(2)}, u32[]{:S(2)}) async-start(bf16[8,512,256]{2,1,0:T(8,128)(2,1)} %get-tuple-element.22), calls=%async_computation.1 | async-start | bytes 4194304 | tf_op jit(solution)/shard_map/all_to_all | solution.py:430
  43.7 21.3 %collective-permute-start.7 = (bf16[128,2048]{1,0:T(8,128)(2,1)}, bf16[128,2048]{1,0:T(8,128)(2,1)}, u32[]{:S(2)}, u32[]{:S(2)}) collective-permute-start(bf16[128,2048]{1,0:T(8,128)(2,1)} %collective-permute-done.4.rest_4_.refs_7_), channel_id=1, source_target_pairs={{0,8},{8,0},{16,24},{24,16},{1,9},{9,1},{17,25},{25,17},{2,10},{10... | collective-permute-start | bytes 1572872 | tf_op jit(solution)/shard_map/ppermute | solution.py:261
  43.8 25.7 %collective-permute-start.6 = (bf16[128,2048]{1,0:T(8,128)(2,1)}, bf16[128,2048]{1,0:T(8,128)(2,1)}, u32[]{:S(2)}, u32[]{:S(2)}) collective-permute-start(bf16[128,2048]{1,0:T(8,128)(2,1)} %collective-permute-done.3.rest_3_.refs_3_), channel_id=1, source_target_pairs={{0,8},{8,0},{16,24},{24,16},{1,9},{9,1},{17,25},{25,17},{2,10},{10... | collective-permute-start | bytes 1572872 | tf_op jit(solution)/shard_map/ppermute | solution.py:261
  70.4 30.2 %all-to-all-start = ((bf16[8,512,256]{2,1,0:T(8,128)(2,1)}), bf16[8,512,256]{2,1,0:T(8,128)(2,1)S(1)}, u32[]{:S(2)}, u32[]{:S(2)}) async-start(bf16[8,512,256]{2,1,0:T(8,128)(2,1)} %get-tuple-element.16), calls=%async_computation | async-start | bytes 4194304 | tf_op jit(solution)/shard_map/all_to_all | solution.py:430
  74.2 2.0 %collective-permute-start.14 = (bf16[128,2048]{1,0:T(8,128)(2,1)S(1)}, bf16[128,2048]{1,0:T(8,128)(2,1)S(1)}, u32[]{:S(2)}, u32[]{:S(2)}) collective-permute-start(bf16[128,2048]{1,0:T(8,128)(2,1)S(1)} %collective-permute-done.5.rest_5_.refs_11_), channel_id=1, source_target_pairs={{0,1},{1,0},{2,3},{3,2},{4,5},{5,4},{6,7},{7,6},{8,9},{9,8},{10,11... | collective-permute-start | bytes 1572872 | tf_op jit(solution)/shard_map/ppermute | solution.py:261
  74.4 14.3 %collective-permute-start.13 = (bf16[128,2048]{1,0:T(8,128)(2,1)S(1)}, bf16[128,2048]{1,0:T(8,128)(2,1)}, u32[]{:S(2)}, u32[]{:S(2)}) collective-permute-start(bf16[128,2048]{1,0:T(8,128)(2,1)S(1)} %collective-permute-done.5.rest_5_.refs_11_), channel_id=1, source_target_pairs={{0,8},{8,0},{16,24},{24,16},{1,9},{9,1},{17,25},{25,17},{2,10},{10... | collective-permute-start | bytes 1572872 | tf_op jit(solution)/shard_map/ppermute | solution.py:261
  74.4 14.4 %collective-permute-start.9 = (bf16[128,2048]{1,0:T(8,128)(2,1)}, bf16[128,2048]{1,0:T(8,128)(2,1)}, u32[]{:S(2)}, u32[]{:S(2)}) collective-permute-start(bf16[128,2048]{1,0:T(8,128)(2,1)} %collective-permute-done.3.rest_3_.refs_3_), channel_id=1, source_target_pairs={{0,1},{1,0},{2,3},{3,2},{4,5},{5,4},{6,7},{7,6},{8,9},{9,8},{10,11... | collective-permute-start | bytes 1572872 | tf_op jit(solution)/shard_map/ppermute | solution.py:261
  74.8 14.0 %collective-permute-start.10 = (bf16[128,2048]{1,0:T(8,128)(2,1)}, bf16[128,2048]{1,0:T(8,128)(2,1)}, u32[]{:S(2)}, u32[]{:S(2)}) collective-permute-start(bf16[128,2048]{1,0:T(8,128)(2,1)} %collective-permute-done.6.refs_4_), channel_id=1, source_target_pairs={{0,1},{1,0},{2,3},{3,2},{4,5},{5,4},{6,7},{7,6},{8,9},{9,8},{10,11... | collective-permute-start | bytes 1572872 | tf_op jit(solution)/shard_map/ppermute | solution.py:261
  74.9 13.9 %collective-permute-start.11 = (bf16[128,2048]{1,0:T(8,128)(2,1)}, bf16[128,2048]{1,0:T(8,128)(2,1)}, u32[]{:S(2)}, u32[]{:S(2)}) collective-permute-start(bf16[128,2048]{1,0:T(8,128)(2,1)} %collective-permute-done.4.rest_4_.refs_7_), channel_id=1, source_target_pairs={{0,1},{1,0},{2,3},{3,2},{4,5},{5,4},{6,7},{7,6},{8,9},{9,8},{10,11... | collective-permute-start | bytes 1572872 | tf_op jit(solution)/shard_map/ppermute | solution.py:261
  76.2 12.6 %collective-permute-start.12 = (bf16[128,2048]{1,0:T(8,128)(2,1)}, bf16[128,2048]{1,0:T(8,128)(2,1)}, u32[]{:S(2)}, u32[]{:S(2)}) collective-permute-start(bf16[128,2048]{1,0:T(8,128)(2,1)} %collective-permute-done.7.refs_8_), channel_id=1, source_target_pairs={{0,1},{1,0},{2,3},{3,2},{4,5},{5,4},{6,7},{7,6},{8,9},{9,8},{10,11... | collective-permute-start | bytes 1572872 | tf_op jit(solution)/shard_map/ppermute | solution.py:261
  88.7 2.3 %collective-permute-start.15 = (bf16[128,2048]{1,0:T(8,128)(2,1)}, bf16[128,2048]{1,0:T(8,128)(2,1)}, u32[]{:S(2)}, u32[]{:S(2)}) collective-permute-start(bf16[128,2048]{1,0:T(8,128)(2,1)} %collective-permute-done.13.refs_12_), channel_id=1, source_target_pairs={{0,1},{1,0},{2,3},{3,2},{4,5},{5,4},{6,7},{7,6},{8,9},{9,8},{10,11... | collective-permute-start | bytes 1572872 | tf_op jit(solution)/shard_map/ppermute | solution.py:261
